TPU v7x, 256 devices: a whole 4x4x8 slice. The times are simulated.
256 devices in a mesh: dp: 4 (over x), pool: 16 (over z, core), head: 4 (over y).
Axes of the slice: x: 4, y: 4, z: 8, core: 2. Of those that a mesh axis runs over, the one named last changes fastest.
Arguments:
- x_prompt: bfloat16 [4, 1024, 4096], P('dp', 'pool'), may hold values from -6 to 6
- x_resp: bfloat16 [4, 4096, 4096], P('dp', 'pool'), may hold values from -6 to 6
- w_kv: bfloat16 [4096, 1024], P(None, 'head'), may hold values from -0.09375 to 0.09375
- q_prompt: bfloat16 [4, 1024, 8192], P('dp', 'pool', 'head'), may hold values from -5 to 5
- q_resp: bfloat16 [4, 4096, 8192], P('dp', 'pool', 'head'), may hold values from -5 to 5
- do_prompt: bfloat16 [4, 1024, 8192], P('dp', 'pool', 'head'), may hold values from -6 to 6
- do_resp: bfloat16 [4, 4096, 8192], P('dp', 'pool', 'head'), may hold values from -6 to 6
- resp_len: int32 [4, 16], P('dp', 'pool'), may hold values from 64 to 256, as said below
Outputs:
- attn_prompt: bfloat16 [4, 1024, 8192], P('dp', 'pool', 'head')
- attn_resp: bfloat16 [4, 4096, 8192], P('dp', 'pool', 'head')
- grad_q_prompt: bfloat16 [4, 1024, 8192], P('dp', 'pool', 'head')
- grad_q_resp: bfloat16 [4, 4096, 8192], P('dp', 'pool', 'head')
- grad_x_prompt: bfloat16 [4, 1024, 4096], P('dp', 'pool', 'head')
- grad_x_resp: bfloat16 [4, 4096, 4096], P('dp', 'pool', 'head')
- grad_w_kv: float32 [4096, 1024], P(('dp', 'pool'), 'head')
Inputs may be any that keep to these rules, and one draw needn't show every extreme that they name: `resp_len`: at least one response in every draw has all 256 tokens live.
All inputs are finite; a program needn't handle non-finite values.
Results may differ from a plain program's by a relative error of at most 0.029.
Values may be sent and summed in bfloat16 or wider, within the bound.
A program may use at most 64 MiB of HBM per device.

v0:
```python
import math

import jax
import jax.numpy as jnp
from jax import lax
from jax.sharding import PartitionSpec as P

HEAD_DIM = 128


def core(query, grad_out, keys, values, allowed):
    scale = 1.0 / math.sqrt(query.shape[-1])
    scores = jnp.dot(query, keys.T, preferred_element_type=jnp.float32) * scale
    expo = jnp.where(allowed, jnp.exp(scores), 0.0)
    weights = expo / jnp.sum(expo, axis=-1, keepdims=True)
    rounded = weights.astype(jnp.bfloat16)
    output = jnp.dot(rounded, values, preferred_element_type=jnp.float32).astype(jnp.bfloat16)
    grad_weights = jnp.dot(grad_out, values.T, preferred_element_type=jnp.float32)
    delta = jnp.sum(
        grad_out.astype(jnp.float32) * output.astype(jnp.float32), axis=-1, keepdims=True
    )
    grad_scores = (weights * (grad_weights - delta)).astype(jnp.bfloat16)
    grad_query = (jnp.dot(grad_scores, keys, preferred_element_type=jnp.float32) * scale).astype(
        jnp.bfloat16
    )
    grad_keys = jnp.dot(grad_scores.T, query, preferred_element_type=jnp.float32) * scale
    grad_values = jnp.dot(rounded.T, grad_out, preferred_element_type=jnp.float32)
    return (output, grad_query, grad_keys, grad_values)


def body(x_prompt, x_resp, w_kv, q_prompt, q_resp, do_prompt, do_resp, resp_len):
    head_size = HEAD_DIM
    width = 2 * head_size
    prompt_rows = x_prompt.shape[1]
    resp_rows = x_resp.shape[1]
    group = q_prompt.shape[2] // head_size
    prompt_hidden = x_prompt[0]
    resp_hidden = x_resp[0]
    kv_resp = jnp.dot(resp_hidden, w_kv, preferred_element_type=jnp.float32).astype(jnp.bfloat16)
    kv_own = jnp.dot(prompt_hidden, w_kv, preferred_element_type=jnp.float32).astype(jnp.bfloat16)
    kv_prompt = lax.all_gather(kv_own, "pool", axis=0, tiled=True)
    full_rows = kv_prompt.shape[0]
    keys_prompt = kv_prompt[:, :head_size]
    values_prompt = kv_prompt[:, head_size:]
    offset = lax.axis_index("pool") * prompt_rows
    prompt_allowed = jnp.arange(full_rows)[None, :] <= (offset + jnp.arange(prompt_rows))[:, None]
    keys_all = jnp.concatenate([keys_prompt, kv_resp[:, :head_size]], axis=0)
    values_all = jnp.concatenate([values_prompt, kv_resp[:, head_size:]], axis=0)
    length = resp_len[0, 0]
    col_ids = jnp.arange(full_rows + resp_rows)[None, :] - full_rows
    row_ids = jnp.arange(resp_rows)[:, None]
    resp_allowed = (col_ids < 0) | (col_ids <= row_ids) & (col_ids < length)
    valid = jnp.arange(resp_rows) < length
    grad_resp_out = jnp.where(valid[:, None], do_resp[0], jnp.zeros_like(do_resp[0]))
    qp_heads = q_prompt[0].reshape(prompt_rows, group, head_size).transpose(1, 0, 2)
    dop_heads = do_prompt[0].reshape(prompt_rows, group, head_size).transpose(1, 0, 2)
    qr_heads = q_resp[0].reshape(resp_rows, group, head_size).transpose(1, 0, 2)
    dor_heads = grad_resp_out.reshape(resp_rows, group, head_size).transpose(1, 0, 2)

    def one_head(acc, parts):
        grad_p, grad_r = acc
        query_p, grad_op, query_r, grad_or = parts
        out_p, dq_p, dk_p, dv_p = core(query_p, grad_op, keys_prompt, values_prompt, prompt_allowed)
        out_r, dq_r, dk_a, dv_a = core(query_r, grad_or, keys_all, values_all, resp_allowed)
        grad_p = grad_p + jnp.concatenate(
            [dk_p + dk_a[:full_rows], dv_p + dv_a[:full_rows]], axis=1
        )
        grad_r = grad_r + jnp.concatenate([dk_a[full_rows:], dv_a[full_rows:]], axis=1)
        return ((grad_p, grad_r), (out_p, out_r, dq_p, dq_r))

    start = (jnp.zeros((full_rows, width), jnp.float32), jnp.zeros((resp_rows, width), jnp.float32))
    (grad_p, grad_r), outs = lax.scan(one_head, start, (qp_heads, dop_heads, qr_heads, dor_heads))
    out_p, out_r, dq_p, dq_r = outs
    owned = lax.psum_scatter(grad_p.astype(jnp.bfloat16), "pool", scatter_dimension=0, tiled=True)
    grad_rb = grad_r.astype(jnp.bfloat16)
    local_w = jnp.dot(prompt_hidden.T, owned, preferred_element_type=jnp.float32) + jnp.dot(
        resp_hidden.T, grad_rb, preferred_element_type=jnp.float32
    )
    grad_w_kv = lax.psum_scatter(local_w, ("dp", "pool"), scatter_dimension=0, tiled=True)
    term_p = jnp.dot(owned, w_kv.T, preferred_element_type=jnp.float32).astype(jnp.bfloat16)
    term_r = jnp.dot(grad_rb, w_kv.T, preferred_element_type=jnp.float32).astype(jnp.bfloat16)
    sum_p, sum_r = (
        lax.psum_scatter(term_p[None], "head", scatter_dimension=2, tiled=True).astype(jnp.float32),
        lax.psum_scatter(term_r[None], "head", scatter_dimension=2, tiled=True).astype(jnp.float32),
    )
    attn_prompt = out_p.transpose(1, 0, 2).reshape(prompt_rows, group * head_size)[None]
    attn_resp = out_r.transpose(1, 0, 2).reshape(resp_rows, group * head_size)[None]
    grad_q_prompt = dq_p.transpose(1, 0, 2).reshape(prompt_rows, group * head_size)[None]
    grad_q_resp = dq_r.transpose(1, 0, 2).reshape(resp_rows, group * head_size)[None]
    return (
        attn_prompt,
        attn_resp,
        grad_q_prompt,
        grad_q_resp,
        sum_p.astype(jnp.bfloat16),
        sum_r.astype(jnp.bfloat16),
        grad_w_kv,
    )


def solution(mesh):
    return jax.shard_map(
        body,
        mesh=mesh,
        in_specs=(
            P("dp", "pool", None),
            P("dp", "pool", None),
            P(None, "head"),
            P("dp", "pool", "head"),
            P("dp", "pool", "head"),
            P("dp", "pool", "head"),
            P("dp", "pool", "head"),
            P("dp", "pool"),
        ),
        out_specs=(
            P("dp", "pool", "head"),
            P("dp", "pool", "head"),
            P("dp", "pool", "head"),
            P("dp", "pool", "head"),
            P("dp", "pool", "head"),
            P("dp", "pool", "head"),
            P(("dp", "pool"), "head"),
        ),
        check_vma=False,
    )
```

profile of v0, /device:TPU:1, one launch (start us, length us, event | category | flops | bytes accessed | tf_op | source)
XLA Modules:
  0.0 562.0 jit_solution(638169125271862607)
XLA Ops:
  9.3 1.5 convolution_convert_fusion.4
  13.4 22.7 %all_gather.3 = bf16[1024,256]{1,0:T(8,128)(2,1)S(1)} all-gather(bf16[64,256]{1,0:T(8,128)(2,1)S(1)} %convolution_convert_fusion.4), channel_id=1, replica_groups=mesh['dp'=4,'pool'=16,'head'=4] {'pool'}, dimensions={0}, use_global_device_ids=true | all-gather | bytes 557056 | tf_op jit(solution)/shard_map/all_gather | solution.py:41
  36.9 2.3 copy.33
  39.1 2.3 copy.34
  41.4 2.3 select_bitcast_fusion
  44.7 249.2 %while.21 = (s32[]{:T(128)}, f32[1024,256]{0,1:T(8,128)S(1)}, f32[256,256]{0,1:T(8,128)}, bf16[16,64,128]{2,1,0:T(8,128)(2,1)}, bf16[16,256,128]{1,2,0:T(8,128)(...) while((s32[]{:T(128)}, f32[1024,256]{0,1:T(8,128)S(1)}, ...), condition=%wide.region_5.6_spmd.clone, body=%wide.region_0.5_spmd.clone.sunk | while | flops 611179904 | bytes 24351380 | solution.py:72
  45.8 1.3 multiply_reduce_fusion.4
  49.7 1.5 fusion.136
  51.2 1.3 multiply_reduce_fusion.5
  61.3 1.3 multiply_reduce_fusion.4
  65.3 1.5 fusion.136
  66.8 1.3 multiply_reduce_fusion.5
  76.9 1.3 multiply_reduce_fusion.4
  80.9 1.5 fusion.136
  82.4 1.3 multiply_reduce_fusion.5
  92.5 1.3 multiply_reduce_fusion.4
  96.4 1.5 fusion.136
  98.0 1.3 multiply_reduce_fusion.5
  108.1 1.3 multiply_reduce_fusion.4
  112.0 1.5 fusion.136
  113.5 1.3 multiply_reduce_fusion.5
  123.6 1.3 multiply_reduce_fusion.4
  127.6 1.5 fusion.136
  129.1 1.3 multiply_reduce_fusion.5
  139.2 1.3 multiply_reduce_fusion.4
  143.2 1.5 fusion.136
  144.7 1.3 multiply_reduce_fusion.5
  154.8 1.3 multiply_reduce_fusion.4
  158.7 1.5 fusion.136
  160.3 1.3 multiply_reduce_fusion.5
  170.4 1.3 multiply_reduce_fusion.4
  174.3 1.5 fusion.136
  175.8 1.3 multiply_reduce_fusion.5
  185.9 1.3 multiply_reduce_fusion.4
  189.9 1.5 fusion.136
  191.4 1.3 multiply_reduce_fusion.5
  201.5 1.3 multiply_reduce_fusion.4
  205.5 1.5 fusion.136
  207.0 1.3 multiply_reduce_fusion.5
  217.1 1.3 multiply_reduce_fusion.4
  221.0 1.5 fusion.136
  222.6 1.3 multiply_reduce_fusion.5
  232.7 1.3 multiply_reduce_fusion.4
  236.6 1.5 fusion.136
  238.2 1.3 multiply_reduce_fusion.5
  248.2 1.3 multiply_reduce_fusion.4
  252.2 1.5 fusion.136
  253.7 1.3 multiply_reduce_fusion.5
  263.8 1.3 multiply_reduce_fusion.4
  267.8 1.5 fusion.136
  269.3 1.3 multiply_reduce_fusion.5
  283.4 1.5 fusion.136
  284.9 1.3 multiply_reduce_fusion.5
  294.8 2.1 copy.45
  296.9 51.4 %reduce-scatter.13.cloned.1.call-done = bf16[64,256]{1,0:T(8,128)(2,1)} async-done(((bf16[1024,256]{1,0:T(8,128)(2,1)}), bf16[64,256]{1,0:T(8,128)(2,1)}) %reduce-scatter.13.cloned.1.call-update) | async-done | bytes 32784
  348.3 2.3 fusion.52
  350.7 2.1 fusion.51
  355.5 2.7 fusion.50
  358.2 5.6 copy.47
  363.8 1.9 copy.42
  371.0 1.4 copy.44
  372.4 2.9 reduce-scatter.9.cloned.1.call-done
  375.3 37.0 %reduce-scatter.11.cloned.1.call-done = bf16[1,256,1024]{2,1,0:T(8,128)(2,1)} async-done(((bf16[1,256,4096]{2,1,0:T(8,128)(2,1)}), bf16[1,256,1024]{2,1,0:T(8,128)(2,1)}) %reduce-scatter.11.cloned.1.call-update) | async-done | bytes 524304 | tf_op jit(solution)/shard_map/reduce_scatter | solution.py:84
  412.3 143.1 %reduce-scatter.15.cloned.1.call-done = f32[64,256]{1,0:T(8,128)} async-done(((f32[4096,256]{1,0:T(8,128)}), f32[64,256]{1,0:T(8,128)}) %reduce-scatter.15.cloned.1.call-update) | async-done | bytes 65552
  (454 shorter events, 196.4 us)
Async XLA Ops:
  7.2 2.1 copy-start
  7.2 341.1 %reduce-scatter.13.cloned.1.call-start = ((), (), s32[]{:S(2)}) async-start(), calls=%async_computation.6 | async-start | bytes 557056
  8.1 2.7 copy-start.6
  10.8 1.8 copy-start.12
  41.4 2.4 copy-start.9
  44.7 5.0 copy-start.14
  44.7 5.0 copy-start.4
  47.1 4.2 copy-start.10
  60.2 5.0 copy-start.14
  60.2 5.0 copy-start.4
  62.6 4.2 copy-start.10
  74.2 1.6 copy-start.2
  75.8 5.0 copy-start.14
  75.8 5.0 copy-start.4
  78.2 4.2 copy-start.10
  91.4 5.0 copy-start.14
  91.4 5.0 copy-start.4
  93.8 4.2 copy-start.10
  107.0 5.0 copy-start.14
  107.0 5.0 copy-start.4
  109.4 4.2 copy-start.10
  120.9 1.6 copy-start.2
  122.5 5.0 copy-start.14
  122.5 5.0 copy-start.4
  124.9 4.2 copy-start.10
  138.1 5.0 copy-start.14
  138.1 5.0 copy-start.4
  140.5 4.2 copy-start.10
  153.7 5.0 copy-start.14
  153.7 5.0 copy-start.4
  156.1 4.2 copy-start.10
  167.7 1.6 copy-start.2
  169.3 5.0 copy-start.14
  169.3 5.0 copy-start.4
  171.7 4.2 copy-start.10
  184.8 5.0 copy-start.14
  184.8 5.0 copy-start.4
  187.2 4.2 copy-start.10
  198.8 1.6 copy-start.2
  200.4 5.0 copy-start.14
  200.4 5.0 copy-start.4
  202.8 4.2 copy-start.10
  214.4 1.6 copy-start.2
  216.0 5.0 copy-start.14
  216.0 5.0 copy-start.4
  218.4 4.2 copy-start.10
  231.6 5.0 copy-start.14
  231.6 5.0 copy-start.4
  234.0 4.2 copy-start.10
  245.5 1.6 copy-start.2
  247.2 5.0 copy-start.14
  247.2 5.0 copy-start.4
  249.6 4.2 copy-start.10
  262.7 5.0 copy-start.14
  262.7 5.0 copy-start.4
  265.1 4.2 copy-start.10
  278.3 5.0 copy-start.14
  278.3 5.0 copy-start.4
  280.7 4.2 copy-start.10
  296.8 53.9 %copy-start.3 = (f32[256,256]{0,1:T(8,128)S(1)}, f32[256,256]{0,1:T(8,128)}, u32[]{:S(2)}) copy-start(f32[256,256]{0,1:T(8,128)} %get-tuple-element.104) | copy-start | bytes 786436
  296.8 78.4 %reduce-scatter.9.cloned.1.call-start = ((), (), s32[]{:S(2)}) async-start(), calls=%async_computation.4 | async-start | bytes 655360 | tf_op jit(solution)/shard_map/reduce_scatter | solution.py:83
  350.6 61.6 %reduce-scatter.11.cloned.1.call-start = ((), (), s32[]{:S(2)}) async-start(), calls=%async_computation.5 | async-start | bytes 2621440 | tf_op jit(solution)/shard_map/reduce_scatter | solution.py:84
  352.9 202.6 %reduce-scatter.15.cloned.1.call-start = ((), (), s32[]{:S(2)}) async-start(), calls=%async_computation.7 | async-start | bytes 4259840
  367.0 4.0 copy-start.8
  (30 other events, 43.4 us)
Sparse Core Ops, SparseCore 0:
  297.0 51.2 reduce-scatter.12
  351.6 23.6 reduce-scatter.8
  378.6 33.6 reduce-scatter.10
  416.8 138.5 reduce-scatter.14
where the time goes:
time: 572 us; the launch traced here: 562 us
  waiting for transfers between devices  234 us (41%)
  matrix products  230 us (40%)
  local copies, waits for them, and re-layouts  45.9 us (8%)
  blocking collectives  22.7 us (4%)
  between operations  14.7 us (3%)
  other arithmetic  12.2 us (2%)
    unnamed x6, waiting for transfers between devices  195 us
    dot_general x32, matrix products, core(): jnp.dot(rounded, values, preferred_element_type=jnp.float32)  41.9 us
    dot_general x32, matrix products, core(): scores = jnp.dot(query, keys.T, preferred_element_type=jnp.float32) * scale  41.8 us
    dot_general x32, matrix products, core(): jnp.dot(grad_out, values.T, preferred_element_type=jnp.float32)  39.1 us
    reduce_scatter x1, waiting for transfers between devices, body(): lax.psum_scatter(term_r[None], 'head', scatter_dimension=2, tiled=True)  37 us
    dot_general x32, matrix products, core(): jnp.dot(rounded.T, grad_out, preferred_element_type=jnp.float32)  34.9 us
    dot_general x32, matrix products, core(): jnp.dot(grad_scores.T, query, preferred_element_type=jnp.float32) * scale  34.2 us
    dot_general x32, matrix products, core(): jnp.dot(grad_scores, keys, preferred_element_type=jnp.float32) * scale  27.8 us
  transfers between devices with their start and end apart: 4, of which 4 were waited for; matrix products, arithmetic and copies ran while one was open for 4% of the time, Pallas kernels for 0%

commit v1 on v0

v1 whole, which is shorter than its diff:
```python
import math

import jax
import jax.numpy as jnp
from jax import lax
from jax.experimental import pallas as pl
from jax.experimental.pallas import tpu as pltpu
from jax.sharding import PartitionSpec as P

HD = 128
LN2 = math.log(2.0)
SCALE = 1.0 / math.sqrt(HD)
KFOLD = SCALE / LN2
F32 = jnp.float32
BF = jnp.bfloat16
MESH = pl.DeviceIdType.MESH
CH = 256
VMEM = pl.BlockSpec(memory_space=pltpu.VMEM)


def dot(a, b):
    return jnp.dot(a, b, preferred_element_type=F32)


def dot_nt(a, b):
    return lax.dot_general(a, b, (((1,), (1,)), ((), ())), preferred_element_type=F32)


def dot_tn(a, b):
    return lax.dot_general(a, b, (((0,), (0,)), ((), ())), preferred_element_type=F32)


def remote(src, dst, send, recv, device):
    return pltpu.make_async_remote_copy(
        src_ref=src, dst_ref=dst, send_sem=send, recv_sem=recv,
        device_id=device, device_id_type=MESH,
    )


def greet(devices):
    barrier = pltpu.get_barrier_semaphore()
    for device in devices:
        pl.semaphore_signal(barrier, inc=1, device_id=device, device_id_type=MESH)
    pl.semaphore_wait(barrier, len(devices))


FAR = (4, 3, 5, 2, 6, 1, 7)
NEAR = (1, 7, 2, 6, 3, 5, 4)


def position():
    d, p, h = lax.axis_index("dp"), lax.axis_index("pool"), lax.axis_index("head")
    return d, p // 2, p % 2, h


def project_kernel(xp, xr, w, kv, send, recv, fsend, frecv):
    d, z, c, h = position()
    at = lambda zz, cc: (d, lax.rem(zz, 8) * 2 + cc, h)
    greet([at(z + k, c) for k in range(1, 8)] + [at(z, 1 - c)])
    lane = lax.broadcasted_iota(jnp.int32, (1, 2 * HD), 1)
    fold = jnp.where(lane < HD, KFOLD, 1.0).astype(F32)
    mine = z * 2 + c
    kv[mine] = (dot(xp[...], w[...]) * fold).astype(BF)
    copies = []
    for k in FAR:
        copy = remote(kv.at[mine], kv.at[mine], send.at[k], recv.at[k], at(z + k, c))
        copy.start()
        copies.append(copy)
    pair = remote(kv.at[mine], kv.at[mine], send.at[0], recv.at[0], at(z, 1 - c))
    pair.start()
    for i in range(4):
        kv[16 + i] = (dot(xr[i * 64:(i + 1) * 64, :], w[...]) * fold).astype(BF)
    forwards = []
    for k in NEAR:
        came = lax.rem(z + 8 - k, 8) * 2 + c
        remote(kv.at[came], kv.at[came], send.at[k], recv.at[k], at(z + k, c)).wait_recv()
        copy = remote(kv.at[came], kv.at[came], fsend.at[k], frecv.at[k], at(z, 1 - c))
        copy.start()
        forwards.append(copy)
    pair.wait()
    for copy in copies:
        copy.wait_send()
    for copy in forwards:
        copy.wait()


def project(xp, xr, w):
    return pl.pallas_call(
        project_kernel,
        in_specs=[VMEM] * 3,
        out_specs=VMEM,
        out_shape=jax.ShapeDtypeStruct((20, 64, 256), BF),
        scratch_shapes=[pltpu.SemaphoreType.DMA((8,))] * 4,
        compiler_params=pltpu.CompilerParams(
            collective_id=0, has_side_effects=True, vmem_limit_bytes=40 << 20
        ),
        cost_estimate=pl.CostEstimate(flops=700_000_000, bytes_accessed=5 << 20, transcendentals=0),
        name="project_gather",
    )(xp, xr, w)


def attend(q, do, kv, acc, e_ref, chunks, mask_of):
    rows = q.shape[0]
    total = jnp.zeros((rows, 128), F32)
    for j in range(chunks):
        at = pl.ds(j * CH, CH)
        e = jnp.exp2(dot_nt(q, kv[at, 0:HD]))
        mask = mask_of(j)
        if mask is not None:
            e = jnp.where(mask, e, 0.0)
        e_ref[:, at] = e
        total = total + e[:, :128] + e[:, 128:]
    inverse = 1.0 / jnp.sum(total, axis=1, keepdims=True)
    out = jnp.zeros((rows, HD), F32)
    for j in range(chunks):
        at = pl.ds(j * CH, CH)
        weights = e_ref[:, at] * inverse
        e_ref[:, at] = weights
        out = out + dot(weights.astype(BF), kv[at, HD:])
    out = out.astype(BF)
    delta = jnp.sum(do.astype(F32) * out.astype(F32), axis=1, keepdims=True)
    grad_q = jnp.zeros((rows, HD), F32)
    for j in range(chunks):
        at = pl.ds(j * CH, CH)
        weights = e_ref[:, at]
        grad_s = (weights * (dot_nt(do, kv[at, HD:]) - delta)).astype(BF)
        grad_q = grad_q + dot(grad_s, kv[at, 0:HD])
        acc[0:HD, at] += dot_tn(q, grad_s)
        acc[HD:, at] += dot_tn(do, weights.astype(BF))
    return out, (grad_q * LN2).astype(BF)


def attention_kernel(scalars, qp, dop, qr, dor, kv, op, gqp, out_r, gqr, dkvp, dkvr, acc, e_ref):
    step = pl.program_id(0)
    length, offset = scalars[0], scalars[1]

    @pl.when(step == 0)
    def _():
        acc[...] = jnp.zeros_like(acc)

    def resp_mask(j):
        if j < 4:
            return None
        row = lax.broadcasted_iota(jnp.int32, (256, CH), 0)
        col = lax.broadcasted_iota(jnp.int32, (256, CH), 1)
        return (col <= row) & (col < length)

    def prompt_mask(j):
        row = lax.broadcasted_iota(jnp.int32, (256, CH), 0) % 64
        col = lax.broadcasted_iota(jnp.int32, (256, CH), 1)
        return col + j * CH <= row + offset

    valid = lax.broadcasted_iota(jnp.int32, (256, HD), 0) < length
    for i in range(4):
        head = slice(i * HD, (i + 1) * HD)
        do = dor[:, head]
        do = jnp.where(valid, do, jnp.zeros_like(do))
        out, grad_q = attend(qr[:, head], do, kv, acc, e_ref, 5, resp_mask)
        out_r[:, head] = out
        gqr[:, head] = grad_q
    q = jnp.concatenate([qp[:, i * HD:(i + 1) * HD] for i in range(4)], axis=0)
    do = jnp.concatenate([dop[:, i * HD:(i + 1) * HD] for i in range(4)], axis=0)
    out, grad_q = attend(q, do, kv, acc, e_ref, 4, prompt_mask)
    for i in range(4):
        op[:, i * HD:(i + 1) * HD] = out[i * 64:(i + 1) * 64]
        gqp[:, i * HD:(i + 1) * HD] = grad_q[i * 64:(i + 1) * 64]

    @pl.when(step == 3)
    def _():
        for j in range(10):
            part = acc[:, pl.ds(j * 128, 128)]
            part = jnp.concatenate([part[:HD] * SCALE, part[HD:]], axis=0).T.astype(BF)
            if j < 8:
                dkvp[0, j] = part[:64]
                dkvp[1, j] = part[64:]
            else:
                dkvr[pl.ds((j - 8) * 128, 128), :] = part


def attention(scalars, qp, dop, qr, dor, kv):
    small = pl.BlockSpec((64, 512), lambda g: (0, g))
    large = pl.BlockSpec((256, 512), lambda g: (0, g))
    return pl.pallas_call(
        attention_kernel,
        grid=(4,),
        in_specs=[
            pl.BlockSpec(memory_space=pltpu.SMEM), small, small, large, large,
            pl.BlockSpec((1280, 256), lambda g: (0, 0)),
        ],
        out_specs=[
            small, small, large, large,
            pl.BlockSpec((2, 8, 64, 256), lambda g: (0, 0, 0, 0)),
            pl.BlockSpec((256, 256), lambda g: (0, 0)),
        ],
        out_shape=[jax.ShapeDtypeStruct((64, 2048), BF)] * 2
        + [jax.ShapeDtypeStruct((256, 2048), BF)] * 2
        + [jax.ShapeDtypeStruct((2, 8, 64, 256), BF), jax.ShapeDtypeStruct((256, 256), BF)],
        scratch_shapes=[pltpu.VMEM((256, 1280), F32), pltpu.VMEM((256, 1280), F32)],
        compiler_params=pltpu.CompilerParams(vmem_limit_bytes=40 << 20),
        cost_estimate=pl.CostEstimate(
            flops=20_000_000_000, bytes_accessed=8 << 20, transcendentals=6_500_000
        ),
        name="attend",
    )(scalars, qp, dop, qr, dor, kv)


def total_of(*parts):
    out = parts[0].astype(F32)
    for part in parts[1:]:
        out = out + part.astype(F32)
    return out


def reduce_kernel(
    xp, xr, dkvp, dkvr, w0, w1, w2, w3, gxp, gxr, gw,
    pair_r, t_s, t_r, own, g_r, g_p, lw, pbuf, prcv, x_s, x_r, z_f, z_s, z_r,
    one_s, one_r, t_ss, t_rs, y_ss, y_rs, yp_ss, yp_rs, p_ss, p_rs, x_ss, x_rs, z_ss, z_rs,
):
    d, z, c, h = position()
    s = 1 - 2 * c
    p = z * 2 + c
    at_z = lambda k: (d, lax.rem(z + k, 8) * 2 + c, h)
    at_x = lambda k: (lax.rem(d + 4 + k, 4), p, h)
    at_y = lambda k: (d, p, lax.rem(h + k, 4))
    sibling = (d, z * 2 + 1 - c, h)
    greet(
        [sibling] + [at_z(k) for k in range(1, 8)] + [at_x(1), at_x(-1)] + [at_y(k) for k in range(1, 4)]
    )
    started = []

    def send(*args):
        copy = remote(*args)
        copy.start()
        started.append(copy)
        return copy

    pair = send(dkvp.at[1 - c], pair_r, one_s.at[0], one_r.at[0], sibling)
    heads = [send(dkvr, g_r.at[k], y_ss.at[k], y_rs.at[k], at_y(k)) for k in (1, 2, 3)]
    pair.wait_recv()
    for b in range(8):
        t_s[b] = total_of(dkvp[c, b], pair_r[b]).astype(BF)
    scatter = []
    for k in FAR:
        to = lax.rem(z + k, 8)
        scatter.append(send(t_s.at[to], t_r.at[k], t_ss.at[k], t_rs.at[k], at_z(k)))
    order = (2, 1, 3, 0)
    for i, r in enumerate(order):
        cols = pl.ds(pl.multiple_of(lax.rem(d + r, 4) * 1024, 1024), 1024)
        lw[i] = dot_tn(xr[:, cols], dkvr[...])
    for copy in scatter:
        copy.wait_recv()
    own[...] = total_of(t_s[z], *[t_r[k] for k in range(1, 8)]).astype(BF)
    owners = [send(own, g_p.at[k], yp_ss.at[k], yp_rs.at[k], at_y(k)) for k in (1, 2, 3)]
    halves = []
    for i, r in enumerate(order):
        cols = pl.ds(pl.multiple_of(lax.rem(d + r, 4) * 1024, 1024), 1024)
        piece = (lw[i] + dot_tn(xp[:, cols], own[...])).astype(BF)
        for b in range(16):
            pbuf[i, b % 2, b // 2] = piece[b * 64:(b + 1) * 64]
        halves.append(send(pbuf.at[i, 1 - c], prcv.at[i], p_ss.at[i], p_rs.at[i], sibling))

    def arrived(i):
        remote(pbuf.at[i, 1 - c], prcv.at[i], p_ss.at[i], p_rs.at[i], sibling).wait_recv()

    direct, summed = 2 - c, 1 + c
    arrived(0)
    x_s[0] = total_of(pbuf[0, c], prcv[0]).astype(BF)
    relay = send(x_s.at[0], x_r.at[0], x_ss.at[0], x_rs.at[0], at_x(s))
    arrived(direct)
    x_s[1] = total_of(pbuf[direct, c], prcv[direct]).astype(BF)
    straight = send(x_s.at[1], x_r.at[1], x_ss.at[1], x_rs.at[1], at_x(-s))
    arrived(summed)
    relay.wait_recv()
    x_s[2] = total_of(pbuf[summed, c], prcv[summed], x_r[0]).astype(BF)
    last = send(x_s.at[2], x_r.at[2], x_ss.at[2], x_rs.at[2], at_x(s))
    for copy in heads:
        copy.wait_recv()
    gxr[...] = (
        dot_nt(dkvr[...], w0[...]) + dot_nt(g_r[1], w1[...]) + dot_nt(g_r[2], w2[...]) + dot_nt(g_r[3], w3[...])
    ).astype(BF)
    arrived(3)
    straight.wait_recv()
    last.wait_recv()
    z_f[...] = total_of(pbuf[3, c], prcv[3], x_r[1], x_r[2])
    z_s[...] = z_f[...].astype(BF)
    final = []
    for k in FAR:
        to = lax.rem(z + k, 8)
        final.append(send(z_s.at[to], z_r.at[k], z_ss.at[k], z_rs.at[k], at_z(k)))
    for copy in owners:
        copy.wait_recv()
    gxp[...] = (
        dot_nt(own[...], w0[...]) + dot_nt(g_p[1], w1[...]) + dot_nt(g_p[2], w2[...]) + dot_nt(g_p[3], w3[...])
    ).astype(BF)
    for copy in final:
        copy.wait_recv()
    gw[...] = total_of(z_f[z], *[z_r[k] for k in range(1, 8)])
    for copy in started:
        copy.wait_send()


def reduce(xp, xr, dkvp, dkvr, ws):
    dma = pltpu.SemaphoreType.DMA
    block = (8, 64, 256)
    return pl.pallas_call(
        reduce_kernel,
        in_specs=[VMEM] * 8,
        out_specs=[VMEM] * 3,
        out_shape=[
            jax.ShapeDtypeStruct((64, 1024), BF),
            jax.ShapeDtypeStruct((256, 1024), BF),
            jax.ShapeDtypeStruct((64, 256), F32),
        ],
        scratch_shapes=[
            pltpu.VMEM(block, BF), pltpu.VMEM(block, BF), pltpu.VMEM(block, BF),
            pltpu.VMEM((64, 256), BF), pltpu.VMEM((4, 256, 256), BF), pltpu.VMEM((4, 64, 256), BF),
            pltpu.VMEM((4, 1024, 256), F32), pltpu.VMEM((4, 2) + block, BF), pltpu.VMEM((4,) + block, BF),
            pltpu.VMEM((3,) + block, BF), pltpu.VMEM((3,) + block, BF),
            pltpu.VMEM(block, F32), pltpu.VMEM(block, BF), pltpu.VMEM(block, BF),
            dma((1,)), dma((1,)), dma((8,)), dma((8,)), dma((4,)), dma((4,)), dma((4,)), dma((4,)),
            dma((4,)), dma((4,)), dma((3,)), dma((3,)), dma((8,)), dma((8,)),
        ],
        compiler_params=pltpu.CompilerParams(
            collective_id=1, has_side_effects=True, vmem_limit_bytes=48 << 20
        ),
        cost_estimate=pl.CostEstimate(flops=1_400_000_000, bytes_accessed=7 << 20, transcendentals=0),
        name="reduce_grads",
    )(xp, xr, dkvp, dkvr, *ws)


def body(x_prompt, x_resp, w_kv, q_prompt, q_resp, do_prompt, do_resp, resp_len):
    h = lax.axis_index("head")
    quarter = lambda k: lax.dynamic_slice(w_kv, (lax.rem(h + k, 4) * 1024, 0), (1024, 256))
    ws = [quarter(0)] + [
        lax.ppermute(quarter(k), "head", [(i, (i + k) % 4) for i in range(4)]) for k in (1, 2, 3)
    ]
    kv = project(x_prompt[0], x_resp[0], w_kv).reshape(1280, 256)
    scalars = jnp.stack([resp_len[0, 0], lax.axis_index("pool") * 64]).astype(jnp.int32)
    op, gqp, out_r, gqr, dkvp, dkvr = attention(
        scalars, q_prompt[0], do_prompt[0], q_resp[0], do_resp[0], kv
    )
    gxp, gxr, gw = reduce(x_prompt[0], x_resp[0], dkvp, dkvr, ws)
    return op[None], out_r[None], gqp[None], gqr[None], gxp[None], gxr[None], gw


def solution(mesh):
    return jax.shard_map(
        body,
        mesh=mesh,
        in_specs=(
            P("dp", "pool", None),
            P("dp", "pool", None),
            P(None, "head"),
            P("dp", "pool", "head"),
            P("dp", "pool", "head"),
            P("dp", "pool", "head"),
            P("dp", "pool", "head"),
            P("dp", "pool"),
        ),
        out_specs=(
            P("dp", "pool", "head"),
            P("dp", "pool", "head"),
            P("dp", "pool", "head"),
            P("dp", "pool", "head"),
            P("dp", "pool", "head"),
            P("dp", "pool", "head"),
            P(("dp", "pool"), "head"),
        ),
        check_vma=False,
    )
```

time: 572 us -> 99.2 us (0.17)
  the two profiles are of different devices: /device:TPU:1 before, /device:TPU:2 now
where the time goes in v1:
time: 99.2 us; the launch traced here: 99 us
  Pallas kernels  85.1 us (86%)
  local copies, waits for them, and re-layouts  6.55 us (7%)
  starting transfers between devices  5.83 us (6%)
  between operations  1.41 us (1%)
    pallas_call x1, Pallas kernels, reduce(): pl.pallas_call(reduce_kernel, in_specs=[VMEM] * 8, out_specs=[VMEM] * 3,...  38.6 us
    pallas_call x1, Pallas kernels, attention(): pl.pallas_call(attention_kernel, grid=(4,), in_specs=[pl.BlockSpec(memory...  31.2 us
    pallas_call x1, Pallas kernels, project(): pl.pallas_call(project_kernel, in_specs=[VMEM] * 3, out_specs=VMEM, out_s...  15.3 us
    ppermute x3, starting transfers between devices, body(): lax.ppermute(quarter(k), 'head', [(i, (i + k) % 4) for i in range(4)])  5.83 us
    unnamed x19, local copies, waits for them, and re-layouts  3.7 us
    dynamic_slice x1, local copies, waits for them, and re-layouts, body(): lax.dynamic_slice(w_kv, (lax.rem(h + k, 4) * 1024, 0), (1024, 256))  2.84 us
  transfers between devices with their start and end apart: 3, of which 0 were waited for; matrix products, arithmetic and copies ran while one was open for 0% of the time, Pallas kernels for 47%

profile of v1, /device:TPU:2, one launch (start us, length us, event | category | flops | bytes accessed | tf_op | source)
XLA Modules:
  0.0 99.0 jit_solution(8406850062840706771)
XLA Ops:
  0.7 0.0 copy-start
  0.7 0.0 copy-start.3
  0.7 2.8 %constant_dynamic-slice_fusion = (bf16[1024,256]{1,0:T(8,128)(2,1)}, bf16[1024,256]{1,0:T(8,128)(2,1)}, bf16[1024,256]{1,0:T(8,128)(2,1)S(1)}, bf16[1024,256]{1,0:T(8,128)(2,1)}) fusion(bf16[4096,256]{1,0:T(8,128)(2,1)} %w.1, s32[]{:T(128)S(6)} %select_n.15, s32[]{:T(128)S(6)} %select_n.13, s32[]{:T(128)S(6)} %select_n.12, s32[]{:T(128)S(6)} %select_n.14), kind=kLoop, calls=%fused_computation | loop fusion | bytes 4194320 | tf_op jit(solution)/shard_map/dynamic_slice | solution.py:333
  3.5 1.6 %collective-permute-start = (bf16[1024,256]{1,0:T(8,128)(2,1)}, bf16[1024,256]{1,0:T(8,128)(2,1)}, u32[]{:S(2)}, u32[]{:S(2)}) collective-permute-start(bf16[1024,256]{1,0:T(8,128)(2,1)} %get-tuple-element.26), channel_id=1, source_target_pairs={{0,1},{1,2},{2,3},{3,0},{4,5},{5,6},{6,7},{7,4},{8,9},{9,10},{10,1... | collective-permute-start | bytes 1572872 | tf_op jit(solution)/shard_map/ppermute | solution.py:335
  5.1 2.9 %collective-permute-start.1 = (bf16[1024,256]{1,0:T(8,128)(2,1)}, bf16[1024,256]{1,0:T(8,128)(2,1)}, u32[]{:S(2)}, u32[]{:S(2)}) collective-permute-start(bf16[1024,256]{1,0:T(8,128)(2,1)} %get-tuple-element.28), channel_id=1, source_target_pairs={{0,2},{1,3},{2,0},{3,1},{4,6},{5,7},{6,4},{7,5},{8,10},{9,11},{10,... | collective-permute-start | bytes 1572872 | tf_op jit(solution)/shard_map/ppermute | solution.py:335
  8.0 1.3 %collective-permute-start.2 = (bf16[1024,256]{1,0:T(8,128)(2,1)}, bf16[1024,256]{1,0:T(8,128)(2,1)}, u32[]{:S(2)}, u32[]{:S(2)}) collective-permute-start(bf16[1024,256]{1,0:T(8,128)(2,1)} %get-tuple-element.25), channel_id=1, source_target_pairs={{0,3},{1,0},{2,1},{3,2},{4,7},{5,4},{6,5},{7,6},{8,11},{9,8},{10,9... | collective-permute-start | bytes 1572872 | tf_op jit(solution)/shard_map/ppermute | solution.py:335
  10.0 0.1 pad_add_fusion.scalars
  10.1 0.0 copy-done
  10.1 0.0 copy-done.3
  10.1 0.0 copy-start.1
  10.1 1.6 %copy-done.1 = bf16[1,256,4096]{2,1,0:T(8,128)(2,1)S(1)} copy-done((bf16[1,256,4096]{2,1,0:T(8,128)(2,1)S(1)}, bf16[1,256,4096]{2,1,0:T(8,128)(2,1)}, u32[]{:S(2)}) %copy-start.1) | copy-done | bytes 2097176
  11.7 0.0 copy-start.4
  11.7 0.0 copy-start.5
  11.7 0.0 copy-start.6
  11.7 0.0 copy-start.7
  11.7 15.3 %project_gather.1 = bf16[20,64,256]{2,1,0:T(8,128)(2,1)S(1)} custom-call(bf16[64,4096]{1,0:T(8,128)(2,1)S(1)} %bitcast.18, bf16[256,4096]{1,0:T(8,128)(2,1)S(1)} %bitcast.16, bf16[4096,256]{1,0:T(8,128)(2,1)S(1)} %copy-done), custom_call_target="tpu_custom_call" | custom-call | flops 700000000 | bytes 5242880 | tf_op jit(solution)/shard_map/project_gather/pallas_call | solution.py:88
  27.0 0.0 copy-done.4
  27.1 0.0 copy-done.5
  27.1 0.0 copy-done.6
  27.1 0.0 copy-done.7
  27.1 0.0 copy-start.2
  27.1 31.2 %attend.1 = (bf16[64,2048]{1,0:T(8,128)(2,1)}, bf16[64,2048]{1,0:T(8,128)(2,1)}, bf16[256,2048]{1,0:T(8,128)(2,1)}, bf16[256,2048]{1,0:T(8,128)(2,1)}, bf16[2,8,...) custom-call(s32[2]{0:T(128)S(1)} %pad_add_fusion.scalars, bf16[64,2048]{1,0:T(8,128)(2,1)S(1)} %bitcast.25, ...), custom_call_target="tpu_custom_call" | custom-call | flops 20000000000 | bytes 8388608 | tf_op jit(solution)/shard_map/attend/pallas_call | solution.py:183
  58.3 0.0 collective-permute-done.w1
  58.3 0.0 collective-permute-done.1.w2
  58.3 0.0 collective-permute-done.2.w3
  58.3 0.0 copy-done.2
  58.3 38.6 %reduce_grads.1 = (bf16[64,1024]{1,0:T(8,128)(2,1)S(1)}, bf16[256,1024]{1,0:T(8,128)(2,1)S(1)}, f32[64,256]{1,0:T(8,128)S(1)}) custom-call(bf16[64,4096]{1,0:T(8,128)(2,1)S(1)} %bitcast.19, bf16[256,4096]{1,0:T(8,128)(2,1)S(1)} %bitcast.17, bf16[2,8,64,256]{3,2,1,0:T(8,128)(2,1)S(1)} %get-tuple-element.20.dkvp, bf16[256,256]{1,0:T(8,128)(2,1)S(1)} %get-tuple-element.21.dkvr, ...), custom_call_target="tpu_custom_call" | custom-call | flops 1400000000 | bytes 7340032 | tf_op jit(solution)/shard_map/reduce_grads/pallas_call | solution.py:305
  96.9 0.7 copy.19
  97.6 0.8 copy.20
  98.4 0.6 copy.21
Async XLA Ops:
  0.7 9.4 %copy-start = (bf16[4096,256]{1,0:T(8,128)(2,1)S(1)}, bf16[4096,256]{1,0:T(8,128)(2,1)}, u32[]{:S(2)}) copy-start(bf16[4096,256]{1,0:T(8,128)(2,1)} %w.1) | copy-start | bytes 6291460
  0.7 9.4 %copy-start.3 = (bf16[1,64,4096]{2,1,0:T(8,128)(2,1)S(1)}, bf16[1,64,4096]{2,1,0:T(8,128)(2,1)}, u32[]{:S(2)}) copy-start(bf16[1,64,4096]{2,1,0:T(8,128)(2,1)} %param.8) | copy-start | bytes 1572868
  3.5 54.8 %collective-permute-start = (bf16[1024,256]{1,0:T(8,128)(2,1)}, bf16[1024,256]{1,0:T(8,128)(2,1)}, u32[]{:S(2)}, u32[]{:S(2)}) collective-permute-start(bf16[1024,256]{1,0:T(8,128)(2,1)} %get-tuple-element.26), channel_id=1, source_target_pairs={{0,1},{1,2},{2,3},{3,0},{4,5},{5,6},{6,7},{7,4},{8,9},{9,10},{10,1... | collective-permute-start | bytes 1572872 | tf_op jit(solution)/shard_map/ppermute | solution.py:335
  5.1 53.2 %collective-permute-start.1 = (bf16[1024,256]{1,0:T(8,128)(2,1)}, bf16[1024,256]{1,0:T(8,128)(2,1)}, u32[]{:S(2)}, u32[]{:S(2)}) collective-permute-start(bf16[1024,256]{1,0:T(8,128)(2,1)} %get-tuple-element.28), channel_id=1, source_target_pairs={{0,2},{1,3},{2,0},{3,1},{4,6},{5,7},{6,4},{7,5},{8,10},{9,11},{10,... | collective-permute-start | bytes 1572872 | tf_op jit(solution)/shard_map/ppermute | solution.py:335
  8.0 50.3 %collective-permute-start.2 = (bf16[1024,256]{1,0:T(8,128)(2,1)}, bf16[1024,256]{1,0:T(8,128)(2,1)}, u32[]{:S(2)}, u32[]{:S(2)}) collective-permute-start(bf16[1024,256]{1,0:T(8,128)(2,1)} %get-tuple-element.25), channel_id=1, source_target_pairs={{0,3},{1,0},{2,1},{3,2},{4,7},{5,4},{6,5},{7,6},{8,11},{9,8},{10,9... | collective-permute-start | bytes 1572872 | tf_op jit(solution)/shard_map/ppermute | solution.py:335
  10.1 1.6 %copy-start.1 = (bf16[1,256,4096]{2,1,0:T(8,128)(2,1)S(1)}, bf16[1,256,4096]{2,1,0:T(8,128)(2,1)}, u32[]{:S(2)}) copy-start(bf16[1,256,4096]{2,1,0:T(8,128)(2,1)} %param.9) | copy-start | bytes 6291460
  11.7 15.4 %copy-start.4 = (bf16[1,256,2048]{2,1,0:T(8,128)(2,1)S(1)}, bf16[1,256,2048]{2,1,0:T(8,128)(2,1)}, u32[]{:S(2)}) copy-start(bf16[1,256,2048]{2,1,0:T(8,128)(2,1)} %param.12) | copy-start | bytes 3145732
  11.7 15.4 %copy-start.5 = (bf16[1,256,2048]{2,1,0:T(8,128)(2,1)S(1)}, bf16[1,256,2048]{2,1,0:T(8,128)(2,1)}, u32[]{:S(2)}) copy-start(bf16[1,256,2048]{2,1,0:T(8,128)(2,1)} %param.14) | copy-start | bytes 3145732
  11.7 15.4 %copy-start.6 = (bf16[1,64,2048]{2,1,0:T(8,128)(2,1)S(1)}, bf16[1,64,2048]{2,1,0:T(8,128)(2,1)}, u32[]{:S(2)}) copy-start(bf16[1,64,2048]{2,1,0:T(8,128)(2,1)} %param.11) | copy-start | bytes 786436
  11.7 15.4 %copy-start.7 = (bf16[1,64,2048]{2,1,0:T(8,128)(2,1)S(1)}, bf16[1,64,2048]{2,1,0:T(8,128)(2,1)}, u32[]{:S(2)}) copy-start(bf16[1,64,2048]{2,1,0:T(8,128)(2,1)} %param.13) | copy-start | bytes 786436
  27.1 31.3 %copy-start.2 = (bf16[1,256,4096]{2,1,0:T(8,128)(2,1)S(1)}, bf16[1,256,4096]{2,1,0:T(8,128)(2,1)}, u32[]{:S(2)}) copy-start(bf16[1,256,4096]{2,1,0:T(8,128)(2,1)} %param.9) | copy-start | bytes 6291460

commit v2 on v0

v2 whole, which is shorter than its diff:
```python
import math

import jax
import jax.numpy as jnp
from jax import lax
from jax.experimental import pallas as pl
from jax.experimental.pallas import tpu as pltpu
from jax.sharding import PartitionSpec as P

HD = 128
LN2 = math.log(2.0)
SCALE = 1.0 / math.sqrt(HD)
KFOLD = SCALE / LN2
F32 = jnp.float32
BF = jnp.bfloat16
MESH = pl.DeviceIdType.MESH
CH = 256
ANY = pl.BlockSpec(memory_space=pl.ANY)


def dot(a, b):
    return jnp.dot(a, b, preferred_element_type=F32)


def dot_nt(a, b):
    return lax.dot_general(a, b, (((1,), (1,)), ((), ())), preferred_element_type=F32)


def dot_tn(a, b):
    return lax.dot_general(a, b, (((0,), (0,)), ((), ())), preferred_element_type=F32)


def remote(src, dst, send, recv, device):
    return pltpu.make_async_remote_copy(
        src_ref=src, dst_ref=dst, send_sem=send, recv_sem=recv,
        device_id=device, device_id_type=MESH,
    )


def greet(devices):
    barrier = pltpu.get_barrier_semaphore()
    for device in devices:
        pl.semaphore_signal(barrier, inc=1, device_id=device, device_id_type=MESH)
    pl.semaphore_wait(barrier, len(devices))


FAR = (4, 3, 5, 2, 6, 1, 7)
NEAR = (1, 7, 2, 6, 3, 5, 4)
ROWS = 1024


def total_of(*parts):
    out = parts[0].astype(F32)
    for part in parts[1:]:
        out = out + part.astype(F32)
    return out


def layer_kernel(
    length_ref, xp_h, xr_h, w_h, qp_h, qr_h, dop_h, dor_h,
    op_h, or_h, gqp_h, gqr_h, gxp_h, gxr_h, gw_h,
    xp, xr, wv, qp, qr, dop, dor, op, out_r, gqp, gqr, gxp, gxr, gw,
    kvp, kvr, kt, xrt, xs, xg, wr,
    ws, e_ref, qs, dos, qts, dots, dl, acc,
    blk, t1r, own, dkg, gp, gr, dkr,
    pbuf, prcv, x_s, x_r, z_f, z_s, z_r, pf, pb, pr,
    loc, kv_ss, kv_rs, f_ss, f_rs, w_ss, w_rs, xg_ss, xg_rs, t_ss, t_rs, a_ss, a_rs,
    y_ss, y_rs, o_ss, o_rs, p_ss, p_rs, x_ss, x_rs, z_ss, z_rs, g_ss, g_rs,
):
    d, h = lax.axis_index("dp"), lax.axis_index("head")
    p = lax.axis_index("pool")
    z, c = p // 2, p % 2
    s = 1 - 2 * c
    at_p = lambda k: (d, lax.rem(p + k, 16), h)
    at_z = lambda k: (d, lax.rem(z + k, 8) * 2 + c, h)
    at_x = lambda k: (lax.rem(d + 4 + k, 4), p, h)
    at_y = lambda k: (d, p, lax.rem(h + k, 4))
    sibling = (d, z * 2 + 1 - c, h)
    started, local = [], []

    def send(*args):
        copy = remote(*args)
        copy.start()
        started.append(copy)
        return copy

    def move(i, a, b):
        copy = pltpu.make_async_copy(a, b, loc.at[i])
        copy.start()
        return copy

    def take(region, sem):
        remote(region, region, z_ss.at[0], sem, sibling).wait_recv()

    loads = [move(i, a, b) for i, (a, b) in enumerate(
        ((xp_h, xp), (w_h, wv), (xr_h, xr), (qr_h, qr), (dor_h, dor), (qp_h, qp), (dop_h, dop)))]
    barrier = pltpu.get_barrier_semaphore()
    peers = [at_p(k) for k in range(1, 16)] + [at_x(k) for k in (1, 2, 3)] + [at_y(k) for k in (1, 2, 3)]
    for peer in peers:
        pl.semaphore_signal(barrier, inc=1, device_id=peer, device_id_type=MESH)

    lane = lax.broadcasted_iota(jnp.int32, (1, 2 * HD), 1)
    fold = jnp.where(lane < HD, KFOLD, 1.0).astype(F32)
    loads[0].wait()
    loads[1].wait()
    mine = (dot(xp[...], wv[...]) * fold).astype(BF)
    for j in range(4):
        kvp[j, p] = mine[16 * j:16 * j + 16]
    pl.semaphore_wait(barrier, len(peers))
    for k in FAR:
        send(kvp.at[:, p], kvp.at[:, p], kv_ss.at[k], kv_rs.at[k], at_z(k))
    send(kvp.at[:, p], kvp.at[:, p], kv_ss.at[0], kv_rs.at[0], sibling)
    for k in (2, 1, 3):
        rows = pl.ds(pl.multiple_of(lax.rem(h + k, 4) * 1024, 1024), 1024)
        send(wv.at[rows], wr.at[k], w_ss.at[k], w_rs.at[k], at_y(k))
    loads[2].wait()
    kvr[...] = (dot(xr[...], wv[...]) * fold).astype(BF)
    kt[:, 1024:] = kvr[...].T
    for b in range(16):
        lanes = [(q * 8 + b // 2) * 128 + (b % 2) * 64 for q in range(4)]
        xs[b] = jnp.concatenate([xp[:, i:i + 64] for i in lanes], axis=1)
    xg[0] = xs[p]
    for i in range(16):
        xrt[i * 256:(i + 1) * 256, :] = xr[:, i * 256:(i + 1) * 256].T
    for k in NEAR:
        came = lax.rem(z + 8 - k, 8) * 2 + c
        take(kvp.at[:, came], kv_rs.at[k])
        send(kvp.at[:, came], kvp.at[:, came], f_ss.at[k], f_rs.at[k], sibling)
    take(kvp.at[:, z * 2 + 1 - c], kv_rs.at[0])
    for k in NEAR:
        take(kvp.at[:, lax.rem(z + 8 - k, 8) * 2 + 1 - c], f_rs.at[k])
    for k in (8, 7, 9, 6, 10, 5, 11, 4, 12, 3, 13, 2, 14, 1, 15):
        send(xs.at[lax.rem(p + k, 16)], xg.at[k], xg_ss.at[k], xg_rs.at[0], at_p(k))
    for j in range(4):
        kt[:, j * CH:(j + 1) * CH] = kvp[j].reshape(CH, 2 * HD).T

    def kv_of(j):
        return kvr[...] if j == 4 else kvp[j].reshape(CH, 2 * HD)

    length, offset = length_ref[0, 0], p * 64

    def forward(start, q, do, chunks, mask_of):
        rows = pl.ds(start, ROWS)
        qs[rows, :] = q
        dos[rows, :] = do
        qts[:, rows] = q.T
        dots[:, rows] = do.T
        total = jnp.zeros((ROWS, 128), F32)
        for j in range(chunks):
            e = jnp.exp2(dot(q, kt[0:HD, j * CH:(j + 1) * CH]))
            mask = mask_of(j)
            if mask is not None:
                e = jnp.where(mask, e, 0.0)
            e_ref[:, j * CH:(j + 1) * CH] = e
            total = total + e[:, :128] + e[:, 128:]
        inverse = 1.0 / jnp.sum(total, axis=1, keepdims=True)
        out = jnp.zeros((ROWS, HD), F32)
        for j in range(chunks):
            weights = (e_ref[:, j * CH:(j + 1) * CH] * inverse).astype(BF)
            ws[rows, j * CH:(j + 1) * CH] = weights
            out = out + dot(weights, kv_of(j)[:, HD:])
        out = out.astype(BF)
        delta = jnp.sum(do.astype(F32) * out.astype(F32), axis=1, keepdims=True)
        dl[rows, :] = jnp.broadcast_to(delta, (ROWS, 128))
        return out

    def resp_mask(j):
        if j < 4:
            return None
        row = lax.broadcasted_iota(jnp.int32, (ROWS, CH), 0) & 255
        col = lax.broadcasted_iota(jnp.int32, (ROWS, CH), 1)
        return (col <= row) & (col < length)

    def prompt_mask(j):
        row = lax.broadcasted_iota(jnp.int32, (ROWS, CH), 0) & 63
        col = lax.broadcasted_iota(jnp.int32, (ROWS, CH), 1)
        return (col >> 4) * 64 + (col & 15) + 16 * j <= row + offset

    valid = lax.broadcasted_iota(jnp.int32, (256, HD), 0) < length
    for copy in loads[3:]:
        copy.wait()

    def resp_block(t, carry):
        heads = [pl.ds(pl.multiple_of((t * 4 + u) * HD, HD), HD) for u in range(4)]
        q = jnp.concatenate([qr[:, head] for head in heads], axis=0)
        do = jnp.concatenate([jnp.where(valid, dor[:, head], jnp.zeros((256, HD), BF)) for head in heads], axis=0)
        out = forward(pl.multiple_of(t * ROWS, ROWS), q, do, 5, resp_mask)
        for u in range(4):
            out_r[:, heads[u]] = out[u * 256:(u + 1) * 256]
        return carry

    lax.fori_loop(0, 4, resp_block, 0)
    local.append(move(7, out_r, or_h))
    q = jnp.concatenate([qp[:, u * HD:(u + 1) * HD] for u in range(16)], axis=0)
    do = jnp.concatenate([dop[:, u * HD:(u + 1) * HD] for u in range(16)], axis=0)
    out = forward(4 * ROWS, q, do, 4, prompt_mask)
    for u in range(16):
        op[:, u * HD:(u + 1) * HD] = out[u * 64:(u + 1) * 64]
    local.append(move(8, op, op_h))

    def backward(j, blocks):
        at = slice(j * CH, (j + 1) * CH)
        acc[...] = jnp.zeros_like(acc)

        def block(t, carry):
            rows = pl.ds(pl.multiple_of(t * ROWS, ROWS), ROWS)
            weights = ws[rows, at]
            delta = dl[rows, :]
            grad_w = dot(dos[rows, :], kt[HD:, at])
            grad_s = (weights.astype(F32) * (grad_w - jnp.concatenate([delta, delta], axis=1))).astype(BF)
            ws[rows, at] = grad_s
            acc[0:HD, :] += dot(qts[:, rows], grad_s)
            acc[HD:, :] += dot(dots[:, rows], weights)
            return carry

        lax.fori_loop(0, blocks, block, 0)
        return jnp.concatenate([acc[0:HD, :] * SCALE, acc[HD:, :]], axis=0).T.astype(BF)

    def scatter(j, part):
        blk[j] = part.reshape(16, 16, 256)
        t1r[j, 0] = blk[j, p]
        for k in (8, 7, 9, 6, 10, 5, 11, 4, 12, 3, 13, 2, 14, 1, 15):
            send(blk.at[j, lax.rem(p + k, 16)], t1r.at[j, k], t_ss.at[j, k], t_rs.at[j], at_p(k))

    def collect(j):
        take(t1r.at[j, pl.ds(1, 15)], t_rs.at[j])
        mine = total_of(*[t1r[j, k] for k in range(16)]).astype(BF)
        own[16 * j:16 * j + 16, :] = mine
        dkg[j, 0] = mine
        rows = pl.ds(16 * j, 16)
        for k in (8, 7, 9, 6, 10, 5, 11, 4, 12, 3, 13, 2, 14, 1, 15):
            send(own.at[rows], dkg.at[j, k], a_ss.at[j, k], a_rs.at[j], at_p(k))
        for k in (1, 2, 3):
            send(own.at[rows], gp.at[k, rows], o_ss.at[j, k], o_rs.at[k], at_y(k))

    dkr[...] = backward(4, 4)
    for k in (1, 2, 3):
        send(dkr, gr.at[k], y_ss.at[k], y_rs.at[k], at_y(k))
    order = (2, 1, 3, 0)
    for i, r in enumerate(order):
        rows = pl.ds(pl.multiple_of(lax.rem(d + r, 4) * 1024, 1024), 1024)
        piece = dot(xrt[rows, :], dkr[...]).astype(BF)
        for b in range(16):
            pbuf[i, b % 2, b // 2] = piece[b * 64:(b + 1) * 64]
        send(pbuf.at[i, 1 - c], prcv.at[i], p_ss.at[i], p_rs.at[i], sibling)
    direct, summed = 2 - c, 1 + c

    scatter(0, backward(0, 5))
    take(prcv.at[0], p_rs.at[0])
    x_s[0] = total_of(pbuf[0, c], prcv[0]).astype(BF)
    send(x_s.at[0], x_r.at[0], x_ss.at[0], x_rs.at[0], at_x(s))
    take(prcv.at[direct], p_rs.at[direct])
    x_s[1] = total_of(pbuf[direct, c], prcv[direct]).astype(BF)
    send(x_s.at[1], x_r.at[1], x_ss.at[1], x_rs.at[1], at_x(-s))

    scatter(1, backward(1, 5))
    collect(0)
    take(prcv.at[summed], p_rs.at[summed])
    take(x_r.at[0], x_rs.at[0])
    x_s[2] = total_of(pbuf[summed, c], prcv[summed], x_r[0]).astype(BF)
    send(x_s.at[2], x_r.at[2], x_ss.at[2], x_rs.at[2], at_x(s))

    scatter(2, backward(2, 5))
    collect(1)
    take(prcv.at[3], p_rs.at[3])
    take(x_r.at[1], x_rs.at[1])
    take(x_r.at[2], x_rs.at[2])
    z_f[...] = total_of(pbuf[3, c], prcv[3], x_r[1], x_r[2])
    z_s[...] = z_f[...].astype(BF)
    for k in FAR:
        send(z_s.at[lax.rem(z + k, 8)], z_r.at[k], z_ss.at[k], z_rs.at[k], at_z(k))

    scatter(3, backward(3, 5))
    collect(2)

    def grad_q_block(t, carry):
        rows = pl.ds(pl.multiple_of(t * ROWS, ROWS), ROWS)
        grad_q = dot(ws[rows, 0:CH], kv_of(0)[:, 0:HD])
        for j in range(1, 5):
            grad_q = grad_q + dot(ws[rows, j * CH:(j + 1) * CH], kv_of(j)[:, 0:HD])
        grad_q = (grad_q * LN2).astype(BF)
        for u in range(4):
            gqr[:, pl.ds(pl.multiple_of((t * 4 + u) * HD, HD), HD)] = grad_q[u * 256:(u + 1) * 256]
        return carry

    lax.fori_loop(0, 2, grad_q_block, 0)
    collect(3)
    lax.fori_loop(2, 4, grad_q_block, 0)
    local.append(move(9, gqr, gqr_h))
    rows = slice(4 * ROWS, 5 * ROWS)
    grad_q = dot(ws[rows, 0:CH], kv_of(0)[:, 0:HD])
    for j in range(1, 4):
        grad_q = grad_q + dot(ws[rows, j * CH:(j + 1) * CH], kv_of(j)[:, 0:HD])
    grad_q = (grad_q * LN2).astype(BF)
    for u in range(16):
        gqp[:, u * HD:(u + 1) * HD] = grad_q[u * 64:(u + 1) * 64]
    local.append(move(10, gqp, gqp_h))

    take(xg.at[pl.ds(1, 15)], xg_rs.at[0])
    share = None
    for j in range(4):
        take(dkg.at[j, pl.ds(1, 15)], a_rs.at[j])
        part = dot_tn(xg[:, 16 * j:16 * j + 16, :].reshape(256, 256), dkg[j].reshape(256, 256))
        share = part if share is None else share + part
    pf[...] = share.reshape(4, 64, 256)
    pb[...] = share.astype(BF).reshape(4, 64, 256)
    for k in (2, 1, 3):
        send(pb.at[lax.rem(d + k, 4)], pr.at[k], g_ss.at[k], g_rs.at[k], at_x(k))

    w_own = wv[pl.ds(pl.multiple_of(h * 1024, 1024), 1024), :]
    for k in (1, 2, 3):
        take(wr.at[k], w_rs.at[k])
        take(gr.at[k], y_rs.at[k])
    gxr[...] = (dot_nt(dkr[...], w_own) + dot_nt(gr[1], wr[1]) + dot_nt(gr[2], wr[2]) + dot_nt(gr[3], wr[3])).astype(BF)
    local.append(move(11, gxr, gxr_h))
    for k in (1, 2, 3):
        take(gp.at[k], o_rs.at[k])
    gxp[...] = (dot_nt(own[...], w_own) + dot_nt(gp[1], wr[1]) + dot_nt(gp[2], wr[2]) + dot_nt(gp[3], wr[3])).astype(BF)
    local.append(move(12, gxp, gxp_h))
    for k in range(1, 8):
        take(z_r.at[k], z_rs.at[k])
    for k in (1, 2, 3):
        take(pr.at[k], g_rs.at[k])
    gw[...] = total_of(z_f[z], pf[d], *[z_r[k] for k in range(1, 8)], *[pr[k] for k in (1, 2, 3)])
    local.append(move(13, gw, gw_h))
    for copy in started:
        copy.wait_send()
    for copy in local:
        copy.wait()


def layer(length, xp, xr, w, qp, qr, dop, dor):
    dma = pltpu.SemaphoreType.DMA
    bf = lambda *shape: pltpu.VMEM(shape, BF)
    f32 = lambda *shape: pltpu.VMEM(shape, F32)
    block = (8, 64, 256)
    outs = [
        jax.ShapeDtypeStruct((64, 2048), BF), jax.ShapeDtypeStruct((256, 2048), BF),
        jax.ShapeDtypeStruct((64, 2048), BF), jax.ShapeDtypeStruct((256, 2048), BF),
        jax.ShapeDtypeStruct((64, 1024), BF), jax.ShapeDtypeStruct((256, 1024), BF),
        jax.ShapeDtypeStruct((64, 256), F32),
    ]
    return pl.pallas_call(
        layer_kernel,
        in_specs=[pl.BlockSpec(memory_space=pltpu.SMEM)] + [ANY] * 7,
        out_specs=[ANY] * 7,
        out_shape=outs,
        scratch_shapes=[
            bf(64, 4096), bf(256, 4096), bf(4096, 256), bf(64, 2048), bf(256, 2048), bf(64, 2048), bf(256, 2048),
            bf(64, 2048), bf(256, 2048), bf(64, 2048), bf(256, 2048), bf(64, 1024), bf(256, 1024), f32(64, 256),
            bf(4, 16, 16, 256), bf(256, 256), bf(256, 1280), bf(4096, 256), bf(16, 64, 256), bf(16, 64, 256),
            bf(4, 1024, 256),
            bf(5120, 1280), f32(ROWS, 1280), bf(5120, HD), bf(5120, HD), bf(HD, 5120), bf(HD, 5120),
            f32(5120, 128), f32(256, 256),
            bf(4, 16, 16, 256), bf(4, 16, 16, 256), bf(64, 256), bf(4, 16, 16, 256), bf(4, 64, 256),
            bf(4, 256, 256), bf(256, 256),
            bf(4, 2, *block), bf(4, *block), bf(3, *block), bf(3, *block), f32(*block), bf(*block), bf(*block),
            f32(4, 64, 256), bf(4, 64, 256), bf(4, 64, 256),
            dma((14,)), dma((8,)), dma((8,)), dma((8,)), dma((8,)), dma((4,)), dma((4,)), dma((16,)), dma((1,)),
            dma((4, 16)), dma((4,)), dma((4, 16)), dma((4,)),
            dma((4,)), dma((4,)), dma((4, 4)), dma((4,)), dma((4,)), dma((4,)), dma((3,)), dma((3,)),
            dma((8,)), dma((8,)), dma((4,)), dma((4,)),
        ],
        compiler_params=pltpu.CompilerParams(
            collective_id=0, has_side_effects=True, vmem_limit_bytes=60 << 20
        ),
        cost_estimate=pl.CostEstimate(
            flops=22_000_000_000, bytes_accessed=12 << 20, transcendentals=6_500_000
        ),
        name="layer",
    )(length, xp, xr, w, qp, qr, dop, dor)


def finish_kernel(*refs):
    n = len(refs) // 2
    sems = refs[-1]
    copies = [pltpu.make_async_copy(refs[i], refs[n + i], sems.at[i]) for i in range(n)]
    for copy in copies:
        copy.start()
    for copy in copies:
        copy.wait()


def finish(arrays):
    return pl.pallas_call(
        finish_kernel,
        in_specs=[ANY] * len(arrays),
        out_specs=[ANY] * len(arrays),
        out_shape=[jax.ShapeDtypeStruct(a.shape, a.dtype) for a in arrays],
        scratch_shapes=[pltpu.SemaphoreType.DMA((len(arrays),))],
        name="finish",
    )(*arrays)


def body(x_prompt, x_resp, w_kv, q_prompt, q_resp, do_prompt, do_resp, resp_len):
    arrays = layer(
        resp_len, x_prompt[0], x_resp[0], w_kv, q_prompt[0], q_resp[0], do_prompt[0], do_resp[0]
    )
    op, out_r, gqp, gqr, gxp, gxr, gw = finish(arrays)
    return op[None], out_r[None], gqp[None], gqr[None], gxp[None], gxr[None], gw


def solution(mesh):
    return jax.shard_map(
        body,
        mesh=mesh,
        in_specs=(
            P("dp", "pool", None),
            P("dp", "pool", None),
            P(None, "head"),
            P("dp", "pool", "head"),
            P("dp", "pool", "head"),
            P("dp", "pool", "head"),
            P("dp", "pool", "head"),
            P("dp", "pool"),
        ),
        out_specs=(
            P("dp", "pool", "head"),
            P("dp", "pool", "head"),
            P("dp", "pool", "head"),
            P("dp", "pool", "head"),
            P("dp", "pool", "head"),
            P("dp", "pool", "head"),
            P(("dp", "pool"), "head"),
        ),
        check_vma=False,
    )
```

time: 572 us -> 183 us (0.32); the launches traced: 562 us -> 183 us
  waiting for transfers between devices: 234 us -> 0 us
  matrix products: 230 us -> 0 us
  Pallas kernels: 0 us -> 181 us
  local copies, waits for them, and re-layouts: 45.9 us -> 0 us
  blocking collectives: 22.7 us -> 0 us
  between operations: 14.7 us -> 1.45 us
  other arithmetic: 12.2 us -> 0 us
    dot_general x198 -> x0, matrix products: 230 us -> none  [the longest x32 41.9 us: core(): jnp.dot(rounded, values, preferred_element_type=jnp.float32)]
    unnamed x6 -> x0, waiting for transfers between devices: 195 us -> none
    pallas_call x0 -> x2, Pallas kernels: none -> 181 us  [the longest x1 102 us: finish(): pl.pallas_call(finish_kernel, in_specs=[ANY] * len(arrays), out_specs=[AN...]
    reduce_scatter x2 -> x0, waiting for transfers between devices: 39.9 us -> none  [the longest x1 37 us: body(): lax.psum_scatter(term_r[None], 'head', scatter_dimension=2, tiled=True)]
    all_gather x1 -> x0, blocking collectives: 22.7 us -> none  [body(): kv_prompt = lax.all_gather(kv_own, 'pool', axis=0, tiled=True)]
    dynamic_update_slice x32 -> x0, local copies, waits for them, and re-layouts: 19.9 us -> none  [body(): lax.scan(one_head, start, (qp_heads, dop_heads, qr_heads, dor_heads))]
    unnamed x28 -> x0, local copies, waits for them, and re-layouts: 15.9 us -> none
    add x33 -> x0, other arithmetic: 6.86 us -> none  [the longest x16 5.72 us: one_head(): grad_p + jnp.concatenate([dk_p + dk_a[:full_rows], dv_p + dv_a[:full_rows...]
  transfers between devices with their start and end apart: 4 -> 0, of which waited for: 4 -> 0; matrix products, arithmetic and copies ran while one was open for 4% -> 0% of each run, Pallas kernels for 0% -> 0%
where the time goes in v2:
time: 183 us
  Pallas kernels  181 us (99%)
    pallas_call x1, Pallas kernels, finish(): pl.pallas_call(finish_kernel, in_specs=[ANY] * len(arrays), out_specs=[AN...  102 us
    pallas_call x1, Pallas kernels, layer(): pl.pallas_call(layer_kernel, in_specs=[pl.BlockSpec(memory_space=pltpu.SM...  78.9 us

profile of v2, /device:TPU:1, one launch (start us, length us, event | category | flops | bytes accessed | tf_op | source)
XLA Modules:
  0.0 182.8 jit_solution(1246375426297942999)
XLA Ops:
  1.3 78.9 %layer.1 = (bf16[64,2048]{1,0:T(8,128)(2,1)}, bf16[256,2048]{1,0:T(8,128)(2,1)}, bf16[64,2048]{1,0:T(8,128)(2,1)}, bf16[256,2048]{1,0:T(8,128)(2,1)}, bf16[64,10...) custom-call(s32[1,1]{1,0:T(1,128)S(6)} %copy.15.length_ref, bf16[64,4096]{1,0:T(8,128)(2,1)} %bitcast.17, ...), custom_call_target="tpu_custom_call" | custom-call | flops 22000001024 | bytes 12582912 | tf_op jit(solution)/shard_map/layer/pallas_call | solution.py:343
  80.2 102.4 %finish.1 = (bf16[64,2048]{1,0:T(8,128)(2,1)}, bf16[256,2048]{1,0:T(8,128)(2,1)}, bf16[64,2048]{1,0:T(8,128)(2,1)}, bf16[256,2048]{1,0:T(8,128)(2,1)}, bf16[64,1...) custom-call(bf16[64,2048]{1,0:T(8,128)(2,1)} %get-tuple-element.21.refs_0_, ...), custom_call_target="tpu_custom_call" | custom-call | tf_op jit(solution)/shard_map/finish/pallas_call | solution.py:385

commit v3 on v2

v3 whole, which is shorter than its diff:
```python
import math

import jax
import jax.numpy as jnp
from jax import lax
from jax.experimental import pallas as pl
from jax.experimental.pallas import tpu as pltpu
from jax.sharding import PartitionSpec as P

HD = 128
LN2 = math.log(2.0)
SCALE = 1.0 / math.sqrt(HD)
KFOLD = SCALE / LN2
F32 = jnp.float32
BF = jnp.bfloat16
MESH = pl.DeviceIdType.MESH
CH = 256
ANY = pl.BlockSpec(memory_space=pl.ANY)


def dot(a, b):
    return jnp.dot(a, b, preferred_element_type=F32)


def dot_nt(a, b):
    return lax.dot_general(a, b, (((1,), (1,)), ((), ())), preferred_element_type=F32)


def dot_tn(a, b):
    return lax.dot_general(a, b, (((0,), (0,)), ((), ())), preferred_element_type=F32)


def remote(src, dst, send, recv, device):
    return pltpu.make_async_remote_copy(
        src_ref=src, dst_ref=dst, send_sem=send, recv_sem=recv,
        device_id=device, device_id_type=MESH,
    )


FAR = (4, 3, 5, 2, 6, 1, 7)
NEAR = (1, 7, 2, 6, 3, 5, 4)
ROWS = 1024
CLUSTER = ((2, 0), (2, 1), (1, 0), (3, 0), (1, 1), (3, 1), (0, 1))


def total_of(*parts):
    out = parts[0].astype(F32)
    for part in parts[1:]:
        out = out + part.astype(F32)
    return out


def layer_kernel(
    length_ref, xp_h, xr_h, w_h, qp_h, qr_h, dop_h, dor_h,
    op_h, or_h, gqp_h, gqr_h, gxp_h, gxr_h, gw_h,
    xp, xr, wv, qp, qr, dop, dor, op, out_r, gqp, gqr, gxp, gxr, gw,
    kvp, kvr, kt, xrt, xs, xg, xgt, wr,
    ws, e_ref, e_own, qs, dos, qts, dots, dl, acc,
    blk, tpr, tsum, t1r, own, og, gp, gr, dkr,
    pbuf, prcv, x_s, x_r, z_f, z_s, z_r,
    loc, kv_ss, kv_rs, f_ss, f_rs, w_ss, w_rs, xg_ss, xg_rs, t_ss, t_rs, a_ss, a_rs,
    y_ss, y_rs, o_ss, o_rs, p_ss, p_rs, x_ss, x_rs, z_ss, z_rs, q_ss, q_rs,
):
    d, h = lax.axis_index("dp"), lax.axis_index("head")
    p = lax.axis_index("pool")
    z, c = p // 2, p % 2
    s = 1 - 2 * c
    at_dc = lambda kd, kc: (lax.rem(d + kd, 4), z * 2 + lax.rem(c + kc, 2), h)
    at_z = lambda k: (d, lax.rem(z + k, 8) * 2 + c, h)
    at_x = lambda k: (lax.rem(d + 4 + k, 4), p, h)
    at_y = lambda k: (d, p, lax.rem(h + k, 4))
    sibling = (d, z * 2 + 1 - c, h)
    started, local = [], []

    def send(*args):
        copy = remote(*args)
        copy.start()
        started.append(copy)
        return copy

    def move(i, a, b):
        copy = pltpu.make_async_copy(a, b, loc.at[i])
        copy.start()
        return copy

    def take(region, sem):
        remote(region, region, z_ss.at[0], sem, sibling).wait_recv()

    loads = [move(i, a, b) for i, (a, b) in enumerate(
        ((xp_h, xp), (w_h, wv), (xr_h, xr), (qr_h, qr), (dor_h, dor), (qp_h, qp), (dop_h, dop)))]
    barrier = pltpu.get_barrier_semaphore()
    peers = [at_z(k) for k in range(1, 8)] + [at_dc(*k) for k in CLUSTER] + [at_y(k) for k in (1, 2, 3)]
    for peer in peers:
        pl.semaphore_signal(barrier, inc=1, device_id=peer, device_id_type=MESH)

    lane = lax.broadcasted_iota(jnp.int32, (1, 2 * HD), 1)
    fold = jnp.where(lane < HD, KFOLD, 1.0).astype(F32)
    loads[0].wait()
    loads[1].wait()
    mine = (dot(xp[...], wv[...]) * fold).astype(BF)
    for j in range(4):
        kvp[j, p] = mine[16 * j:16 * j + 16]
    pl.semaphore_wait(barrier, len(peers))
    for k in FAR:
        send(kvp.at[:, p], kvp.at[:, p], kv_ss.at[k], kv_rs.at[k], at_z(k))
    send(kvp.at[:, p], kvp.at[:, p], kv_ss.at[0], kv_rs.at[0], sibling)
    for k in (2, 1, 3):
        rows = pl.ds(pl.multiple_of(lax.rem(h + k, 4) * 1024, 1024), 1024)
        send(wv.at[rows], wr.at[k], w_ss.at[k], w_rs.at[k], at_y(k))
    loads[2].wait()
    kvr[...] = (dot(xr[...], wv[...]) * fold).astype(BF)
    kt[:, 1024:] = kvr[...].T
    for q in range(4):
        for half in range(2):
            starts = [q * 1024 + b * 128 + half * 64 for b in range(8)]
            xs[q, half] = jnp.concatenate([xp[:, i:i + 64] for i in starts], axis=1)
    xg[0, 0] = xs[d, c]
    for kd, kc in CLUSTER:
        send(xs.at[lax.rem(d + kd, 4), lax.rem(c + kc, 2)], xg.at[kd, kc], xg_ss.at[kd, kc], xg_rs.at[kd, kc], at_dc(kd, kc))
    for i in range(16):
        xrt[i * 256:(i + 1) * 256, :] = xr[:, i * 256:(i + 1) * 256].T
    for copy in loads[3:]:
        copy.wait()
    length, offset = length_ref[0, 0], p * 64
    row = lax.broadcasted_iota(jnp.int32, (ROWS, CH), 0)
    col = lax.broadcasted_iota(jnp.int32, (ROWS, CH), 1)
    resp_mask = (col <= (row & 255)) & (col < length)
    valid = lax.broadcasted_iota(jnp.int32, (256, HD), 0) < length

    def keep(t, q, do):
        rows = slice(t * ROWS, (t + 1) * ROWS)
        qs[rows, :] = q
        dos[rows, :] = do
        qts[:, rows] = q.T
        dots[:, rows] = do.T

    for t in range(4):
        heads = [slice((t * 4 + u) * HD, (t * 4 + u + 1) * HD) for u in range(4)]
        q = jnp.concatenate([qr[:, head] for head in heads], axis=0)
        do = jnp.concatenate([jnp.where(valid, dor[:, head], jnp.zeros((256, HD), BF)) for head in heads], axis=0)
        keep(t, q, do)
        e_own[t * ROWS:(t + 1) * ROWS, :] = jnp.where(resp_mask, jnp.exp2(dot(q, kt[0:HD, 1024:])), 0.0)
    q = jnp.concatenate([qp[:, u * HD:(u + 1) * HD] for u in range(16)], axis=0)
    do = jnp.concatenate([dop[:, u * HD:(u + 1) * HD] for u in range(16)], axis=0)
    keep(4, q, do)
    for k in NEAR:
        came = lax.rem(z + 8 - k, 8) * 2 + c
        take(kvp.at[:, came], kv_rs.at[k])
        send(kvp.at[:, came], kvp.at[:, came], f_ss.at[k], f_rs.at[k], sibling)
    take(kvp.at[:, z * 2 + 1 - c], kv_rs.at[0])
    for k in NEAR:
        take(kvp.at[:, lax.rem(z + 8 - k, 8) * 2 + 1 - c], f_rs.at[k])
    for j in range(4):
        kt[:, j * CH:(j + 1) * CH] = kvp[j].reshape(CH, 2 * HD).T

    def kv_of(j):
        return kvr[...] if j == 4 else kvp[j].reshape(CH, 2 * HD)

    def forward(t):
        rows = slice(t * ROWS, (t + 1) * ROWS)
        q, do = qs[rows, :], dos[rows, :]
        total = jnp.zeros((ROWS, 128), F32)
        for j in range(4):
            e = jnp.exp2(dot(q, kt[0:HD, j * CH:(j + 1) * CH]))
            if t == 4:
                allowed = (col >> 4) * 64 + (col & 15) + 16 * j <= (row & 63) + offset
                e = jnp.where(allowed, e, 0.0)
            e_ref[:, j * CH:(j + 1) * CH] = e
            total = total + e[:, :128] + e[:, 128:]
        if t < 4:
            total = total + e_own[rows, :128] + e_own[rows, 128:]
        inverse = 1.0 / jnp.sum(total, axis=1, keepdims=True)
        out = jnp.zeros((ROWS, HD), F32)
        for j in range(4 if t == 4 else 5):
            e = e_own[rows, :] if j == 4 else e_ref[:, j * CH:(j + 1) * CH]
            weights = (e * inverse).astype(BF)
            ws[rows, j * CH:(j + 1) * CH] = weights
            out = out + dot(weights, kv_of(j)[:, HD:])
        out = out.astype(BF)
        delta = jnp.sum(do.astype(F32) * out.astype(F32), axis=1, keepdims=True)
        dl[rows, :] = jnp.broadcast_to(delta, (ROWS, 128))
        return out

    for t in range(4):
        out = forward(t)
        for u in range(4):
            out_r[:, (t * 4 + u) * HD:(t * 4 + u + 1) * HD] = out[u * 256:(u + 1) * 256]
    local.append(move(7, out_r, or_h))

    def backward(j, blocks):
        at = slice(j * CH, (j + 1) * CH)
        acc[...] = jnp.zeros_like(acc)

        for t in range(blocks):
            rows = slice(t * ROWS, (t + 1) * ROWS)
            weights = ws[rows, at]
            delta = dl[rows, :]
            grad_w = dot(dos[rows, :], kt[HD:, at])
            grad_s = (weights.astype(F32) * (grad_w - jnp.concatenate([delta, delta], axis=1))).astype(BF)
            ws[rows, at] = grad_s
            acc[0:HD, :] += dot(qts[:, rows], grad_s)
            acc[HD:, :] += dot(dots[:, rows], weights)
        return jnp.concatenate([acc[0:HD, :] * SCALE, acc[HD:, :]], axis=0).T.astype(BF)

    def pair_up(j, part):
        for b in range(16):
            blk[j, b % 2, b // 2] = part[b * 16:(b + 1) * 16]
        send(blk.at[j, 1 - c], tpr.at[j], q_ss.at[j], q_rs.at[j], sibling)

    def scatter(j):
        take(tpr.at[j], q_rs.at[j])
        tsum[j] = total_of(blk[j, c], tpr[j]).astype(BF)
        for k in FAR:
            send(tsum.at[j, lax.rem(z + k, 8)], t1r.at[j, k], t_ss.at[j, k], t_rs.at[j, k], at_z(k))

    def collect(j):
        for k in NEAR:
            take(t1r.at[j, k], t_rs.at[j, k])
        mine = total_of(tsum[j, z], *[t1r[j, k] for k in range(1, 8)]).astype(BF)
        rows = slice(16 * j, 16 * j + 16)
        own[rows, :] = mine
        og[0, 0, rows] = mine
        rows = pl.ds(16 * j, 16)
        for kd, kc in CLUSTER:
            send(own.at[rows], og.at[kd, kc, rows], a_ss.at[j, kd, kc], a_rs.at[j, kd, kc], at_dc(kd, kc))
        for k in (1, 2, 3):
            send(own.at[rows], gp.at[k, rows], o_ss.at[j, k], o_rs.at[k], at_y(k))

    dkr[...] = backward(4, 4)
    for k in (1, 2, 3):
        send(dkr, gr.at[k], y_ss.at[k], y_rs.at[k], at_y(k))
    order = (2, 1, 3, 0)
    for i, r in enumerate(order):
        rows = pl.ds(pl.multiple_of(lax.rem(d + r, 4) * 1024, 1024), 1024)
        piece = dot(xrt[rows, :], dkr[...]).astype(BF)
        for b in range(16):
            pbuf[i, b % 2, b // 2] = piece[b * 64:(b + 1) * 64]
        send(pbuf.at[i, 1 - c], prcv.at[i], p_ss.at[i], p_rs.at[i], sibling)
    direct, summed = 2 - c, 1 + c
    out = forward(4)
    for u in range(16):
        op[:, u * HD:(u + 1) * HD] = out[u * 64:(u + 1) * 64]
    local.append(move(8, op, op_h))
    take(prcv.at[0], p_rs.at[0])
    x_s[0] = total_of(pbuf[0, c], prcv[0]).astype(BF)
    send(x_s.at[0], x_r.at[0], x_ss.at[0], x_rs.at[0], at_x(s))

    pair_up(0, backward(0, 5))
    take(prcv.at[direct], p_rs.at[direct])
    x_s[1] = total_of(pbuf[direct, c], prcv[direct]).astype(BF)
    send(x_s.at[1], x_r.at[1], x_ss.at[1], x_rs.at[1], at_x(-s))

    pair_up(1, backward(1, 5))
    scatter(0)
    pair_up(2, backward(2, 5))
    scatter(1)
    take(prcv.at[summed], p_rs.at[summed])
    take(x_r.at[0], x_rs.at[0])
    x_s[2] = total_of(pbuf[summed, c], prcv[summed], x_r[0]).astype(BF)
    send(x_s.at[2], x_r.at[2], x_ss.at[2], x_rs.at[2], at_x(s))
    pair_up(3, backward(3, 5))
    scatter(2)
    collect(0)

    def grad_q_block(t):
        rows = slice(t * ROWS, (t + 1) * ROWS)
        grad_q = dot(ws[rows, 0:CH], kv_of(0)[:, 0:HD])
        for j in range(1, 5):
            grad_q = grad_q + dot(ws[rows, j * CH:(j + 1) * CH], kv_of(j)[:, 0:HD])
        grad_q = (grad_q * LN2).astype(BF)
        for u in range(4):
            gqr[:, (t * 4 + u) * HD:(t * 4 + u + 1) * HD] = grad_q[u * 256:(u + 1) * 256]

    grad_q_block(0)
    grad_q_block(1)
    scatter(3)
    collect(1)
    grad_q_block(2)
    collect(2)
    grad_q_block(3)
    local.append(move(9, gqr, gqr_h))
    rows = slice(4 * ROWS, 5 * ROWS)
    grad_q = dot(ws[rows, 0:CH], kv_of(0)[:, 0:HD])
    for j in range(1, 4):
        grad_q = grad_q + dot(ws[rows, j * CH:(j + 1) * CH], kv_of(j)[:, 0:HD])
    grad_q = (grad_q * LN2).astype(BF)
    for u in range(16):
        gqp[:, u * HD:(u + 1) * HD] = grad_q[u * 64:(u + 1) * 64]
    local.append(move(10, gqp, gqp_h))
    collect(3)

    for kd, kc in CLUSTER:
        take(xg.at[kd, kc], xg_rs.at[kd, kc])
    xgt[...] = xg[...].reshape(512, 512).T
    take(prcv.at[3], p_rs.at[3])
    take(x_r.at[1], x_rs.at[1])
    take(x_r.at[2], x_rs.at[2])
    z_f[...] = total_of(pbuf[3, c], prcv[3], x_r[1], x_r[2])
    for j in range(4):
        for kd, kc in CLUSTER:
            take(og.at[kd, kc, pl.ds(16 * j, 16)], a_rs.at[j, kd, kc])
    z_f[...] += dot(xgt[...], og[...].reshape(512, 256)).reshape(8, 64, 256)
    z_s[...] = z_f[...].astype(BF)
    for k in FAR:
        send(z_s.at[lax.rem(z + k, 8)], z_r.at[k], z_ss.at[k], z_rs.at[k], at_z(k))

    w_own = wv[pl.ds(pl.multiple_of(h * 1024, 1024), 1024), :]
    for k in (1, 2, 3):
        take(wr.at[k], w_rs.at[k])
        take(gr.at[k], y_rs.at[k])
    gxr[...] = (dot_nt(dkr[...], w_own) + dot_nt(gr[1], wr[1]) + dot_nt(gr[2], wr[2]) + dot_nt(gr[3], wr[3])).astype(BF)
    local.append(move(11, gxr, gxr_h))
    for k in (1, 2, 3):
        take(gp.at[k], o_rs.at[k])
    gxp[...] = (dot_nt(own[...], w_own) + dot_nt(gp[1], wr[1]) + dot_nt(gp[2], wr[2]) + dot_nt(gp[3], wr[3])).astype(BF)
    local.append(move(12, gxp, gxp_h))
    for k in range(1, 8):
        take(z_r.at[k], z_rs.at[k])
    gw[...] = total_of(z_f[z], *[z_r[k] for k in range(1, 8)])
    local.append(move(13, gw, gw_h))
    for copy in started:
        copy.wait_send()
    for copy in local:
        copy.wait()


def layer(length, xp, xr, w, qp, qr, dop, dor):
    dma = pltpu.SemaphoreType.DMA
    bf = lambda *shape: pltpu.VMEM(shape, BF)
    f32 = lambda *shape: pltpu.VMEM(shape, F32)
    block = (8, 64, 256)
    outs = [
        jax.ShapeDtypeStruct((64, 2048), BF), jax.ShapeDtypeStruct((256, 2048), BF),
        jax.ShapeDtypeStruct((64, 2048), BF), jax.ShapeDtypeStruct((256, 2048), BF),
        jax.ShapeDtypeStruct((64, 1024), BF), jax.ShapeDtypeStruct((256, 1024), BF),
        jax.ShapeDtypeStruct((64, 256), F32),
    ]
    return pl.pallas_call(
        layer_kernel,
        in_specs=[pl.BlockSpec(memory_space=pltpu.SMEM)] + [ANY] * 7,
        out_specs=[ANY] * 7,
        out_shape=outs,
        scratch_shapes=[
            bf(64, 4096), bf(256, 4096), bf(4096, 256), bf(64, 2048), bf(256, 2048), bf(64, 2048), bf(256, 2048),
            bf(64, 2048), bf(256, 2048), bf(64, 2048), bf(256, 2048), bf(64, 1024), bf(256, 1024), f32(64, 256),
            bf(4, 16, 16, 256), bf(256, 256), bf(256, 1280), bf(4096, 256), bf(4, 2, 64, 512), bf(4, 2, 64, 512),
            bf(512, 512),            bf(4, 1024, 256),
            bf(5120, 1280), f32(ROWS, 1024), f32(4 * ROWS, CH), bf(5120, HD), bf(5120, HD), bf(HD, 5120), bf(HD, 5120),
            f32(5120, 128), f32(256, 256),
            bf(4, 2, 8, 16, 256), bf(4, 8, 16, 256), bf(4, 8, 16, 256), bf(4, 8, 16, 256), bf(64, 256),
            bf(4, 2, 64, 256), bf(4, 64, 256),
            bf(4, 256, 256), bf(256, 256),
            bf(4, 2, *block), bf(4, *block), bf(3, *block), bf(3, *block), f32(*block), bf(*block), bf(*block),
            dma((14,)), dma((8,)), dma((8,)), dma((8,)), dma((8,)), dma((4,)), dma((4,)), dma((4, 2)), dma((4, 2)),
            dma((4, 8)), dma((4, 8)), dma((4, 4, 2)), dma((4, 4, 2)),
            dma((4,)), dma((4,)), dma((4, 4)), dma((4,)), dma((4,)), dma((4,)), dma((3,)), dma((3,)),
            dma((8,)), dma((8,)), dma((4,)), dma((4,)),
        ],
        compiler_params=pltpu.CompilerParams(
            collective_id=0, has_side_effects=True, vmem_limit_bytes=60 << 20
        ),
        cost_estimate=pl.CostEstimate(
            flops=22_000_000_000, bytes_accessed=12 << 20, transcendentals=6_500_000
        ),
        name="layer",
    )(length, xp, xr, w, qp, qr, dop, dor)


def finish_kernel(*refs):
    n = len(refs[:-2]) // 3
    came, went = refs[-2:]
    ins, outs, held = refs[:n], refs[n:2 * n], refs[2 * n:3 * n]
    reads = [pltpu.make_async_copy(ins[i], held[i], came.at[i]) for i in range(n)]
    writes = [pltpu.make_async_copy(held[i], outs[i], went.at[i]) for i in range(n)]
    for copy in reads:
        copy.start()
    for i in range(n):
        reads[i].wait()
        writes[i].start()
    for copy in writes:
        copy.wait()


def finish(arrays):
    n = len(arrays)
    return pl.pallas_call(
        finish_kernel,
        in_specs=[ANY] * n,
        out_specs=[ANY] * n,
        out_shape=[jax.ShapeDtypeStruct(a.shape, a.dtype) for a in arrays],
        scratch_shapes=[pltpu.VMEM(a.shape, a.dtype) for a in arrays] + [pltpu.SemaphoreType.DMA((n,))] * 2,
        name="finish",
    )(*arrays)


def body(x_prompt, x_resp, w_kv, q_prompt, q_resp, do_prompt, do_resp, resp_len):
    arrays = layer(
        resp_len, x_prompt[0], x_resp[0], w_kv, q_prompt[0], q_resp[0], do_prompt[0], do_resp[0]
    )
    op, out_r, gqp, gqr, gxp, gxr, gw = finish(arrays)
    return op[None], out_r[None], gqp[None], gqr[None], gxp[None], gxr[None], gw


def solution(mesh):
    return jax.shard_map(
        body,
        mesh=mesh,
        in_specs=(
            P("dp", "pool", None),
            P("dp", "pool", None),
            P(None, "head"),
            P("dp", "pool", "head"),
            P("dp", "pool", "head"),
            P("dp", "pool", "head"),
            P("dp", "pool", "head"),
            P("dp", "pool"),
        ),
        out_specs=(
            P("dp", "pool", "head"),
            P("dp", "pool", "head"),
            P("dp", "pool", "head"),
            P("dp", "pool", "head"),
            P("dp", "pool", "head"),
            P("dp", "pool", "head"),
            P(("dp", "pool"), "head"),
        ),
        check_vma=False,
    )
```

time: 183 us -> 63.3 us (0.35)
  Pallas kernels: 181 us -> 61.7 us
    pallas_call x1, Pallas kernels: 102 us -> 3.06 us  [finish(): pl.pallas_call(finish_kernel, in_specs=[ANY] * n, out_specs=[ANY] * n, ou...]
    pallas_call x1, Pallas kernels: 78.9 us -> 58.7 us  [layer(): pl.pallas_call(layer_kernel, in_specs=[pl.BlockSpec(memory_space=pltpu.SM...]
where the time goes in v3:
time: 63.3 us; the launch traced here: 63.2 us
  Pallas kernels  61.7 us (97%)
  between operations  1.45 us (2%)
    pallas_call x1, Pallas kernels, layer(): pl.pallas_call(layer_kernel, in_specs=[pl.BlockSpec(memory_space=pltpu.SM...  58.7 us
    pallas_call x1, Pallas kernels, finish(): pl.pallas_call(finish_kernel, in_specs=[ANY] * n, out_specs=[ANY] * n, ou...  3.06 us

profile of v3, /device:TPU:1, one launch (start us, length us, event | category | flops | bytes accessed | tf_op | source)
XLA Modules:
  0.0 63.2 jit_solution(763430699104870563)
XLA Ops:
  1.3 58.7 %layer.1 = (bf16[64,2048]{1,0:T(8,128)(2,1)}, bf16[256,2048]{1,0:T(8,128)(2,1)}, bf16[64,2048]{1,0:T(8,128)(2,1)}, bf16[256,2048]{1,0:T(8,128)(2,1)}, bf16[64,10...) custom-call(s32[1,1]{1,0:T(1,128)S(6)} %copy.15.length_ref, bf16[64,4096]{1,0:T(8,128)(2,1)} %bitcast.17, ...), custom_call_target="tpu_custom_call" | custom-call | flops 22000001024 | bytes 12582912 | tf_op jit(solution)/shard_map/layer/pallas_call | solution.py:338
  59.9 3.1 %finish.1 = (bf16[64,2048]{1,0:T(8,128)(2,1)}, bf16[256,2048]{1,0:T(8,128)(2,1)}, bf16[64,2048]{1,0:T(8,128)(2,1)}, bf16[256,2048]{1,0:T(8,128)(2,1)}, bf16[64,1...) custom-call(bf16[64,2048]{1,0:T(8,128)(2,1)} %get-tuple-element.21.refs_0_, ...), custom_call_target="tpu_custom_call" | custom-call | tf_op jit(solution)/shard_map/finish/pallas_call | solution.py:386

commit v4 on v3

--- a/solution.py
+++ b/solution.py
@@ -51,13 +51,13 @@
 
 
 def layer_kernel(
-    length_ref, xp_h, xr_h, w_h, qp_h, qr_h, dop_h, dor_h,
+    length_h, xp_h, xr_h, w_h, qp_h, qr_h, dop_h, dor_h,
     op_h, or_h, gqp_h, gqr_h, gxp_h, gxr_h, gw_h,
-    xp, xr, wv, qp, qr, dop, dor, op, out_r, gqp, gqr, gxp, gxr, gw,
+    length_ref, xp, xr, wv, qp, qr, dop, dor, op, out_r, gqp, gqr, gxp, gxr, gw,
     kvp, kvr, kt, xrt, xs, xg, xgt, wr,
     ws, e_ref, e_own, qs, dos, qts, dots, dl, acc,
     blk, tpr, tsum, t1r, own, og, gp, gr, dkr,
-    pbuf, prcv, x_s, x_r, z_f, z_s, z_r,
+    pbuf, prcv, x_s, x_r, z_f, z_s, z_r, z_m,
     loc, kv_ss, kv_rs, f_ss, f_rs, w_ss, w_rs, xg_ss, xg_rs, t_ss, t_rs, a_ss, a_rs,
     y_ss, y_rs, o_ss, o_rs, p_ss, p_rs, x_ss, x_rs, z_ss, z_rs, q_ss, q_rs,
 ):
@@ -66,7 +66,7 @@
     z, c = p // 2, p % 2
     s = 1 - 2 * c
     at_dc = lambda kd, kc: (lax.rem(d + kd, 4), z * 2 + lax.rem(c + kc, 2), h)
-    at_z = lambda k: (d, lax.rem(z + k, 8) * 2 + c, h)
+    at_z = lambda k: (d, lax.rem(z + 8 + k, 8) * 2 + c, h)
     at_x = lambda k: (lax.rem(d + 4 + k, 4), p, h)
     at_y = lambda k: (d, p, lax.rem(h + k, 4))
     sibling = (d, z * 2 + 1 - c, h)
@@ -87,7 +87,7 @@
         remote(region, region, z_ss.at[0], sem, sibling).wait_recv()
 
     loads = [move(i, a, b) for i, (a, b) in enumerate(
-        ((xp_h, xp), (w_h, wv), (xr_h, xr), (qr_h, qr), (dor_h, dor), (qp_h, qp), (dop_h, dop)))]
+        ((xp_h, xp), (w_h, wv), (xr_h, xr), (qr_h, qr), (dor_h, dor), (qp_h, qp), (dop_h, dop), (length_h, length_ref)))]
     barrier = pltpu.get_barrier_semaphore()
     peers = [at_z(k) for k in range(1, 8)] + [at_dc(*k) for k in CLUSTER] + [at_y(k) for k in (1, 2, 3)]
     for peer in peers:
@@ -101,7 +101,7 @@
     for j in range(4):
         kvp[j, p] = mine[16 * j:16 * j + 16]
     pl.semaphore_wait(barrier, len(peers))
-    for k in FAR:
+    for k in (2, 6, 1, 7):
         send(kvp.at[:, p], kvp.at[:, p], kv_ss.at[k], kv_rs.at[k], at_z(k))
     send(kvp.at[:, p], kvp.at[:, p], kv_ss.at[0], kv_rs.at[0], sibling)
     for k in (2, 1, 3):
@@ -143,10 +143,15 @@
     q = jnp.concatenate([qp[:, u * HD:(u + 1) * HD] for u in range(16)], axis=0)
     do = jnp.concatenate([dop[:, u * HD:(u + 1) * HD] for u in range(16)], axis=0)
     keep(4, q, do)
-    for k in NEAR:
-        came = lax.rem(z + 8 - k, 8) * 2 + c
-        take(kvp.at[:, came], kv_rs.at[k])
-        send(kvp.at[:, came], kvp.at[:, came], f_ss.at[k], f_rs.at[k], sibling)
+    came = lambda k: kvp.at[:, lax.rem(z + 16 - k, 8) * 2 + c]
+    for k, to in ((2, 1), (6, -1)):
+        take(came(k), kv_rs.at[k])
+        send(came(k), came(k), kv_ss.at[4 - to], kv_rs.at[4 - to], at_z(to))
+    send(came(2 * s), came(2 * s), kv_ss.at[4], kv_rs.at[4], at_z(2 * s))
+    for k in (2, 6, 1, 7, 3, 5, 4):
+        if k not in (2, 6):
+            take(came(k), kv_rs.at[k])
+        send(came(k), came(k), f_ss.at[k], f_rs.at[k], sibling)
     take(kvp.at[:, z * 2 + 1 - c], kv_rs.at[0])
     for k in NEAR:
         take(kvp.at[:, lax.rem(z + 8 - k, 8) * 2 + 1 - c], f_rs.at[k])
@@ -185,7 +190,7 @@
         out = forward(t)
         for u in range(4):
             out_r[:, (t * 4 + u) * HD:(t * 4 + u + 1) * HD] = out[u * 256:(u + 1) * 256]
-    local.append(move(7, out_r, or_h))
+    local.append(move(14, out_r, or_h))
 
     def backward(j, blocks):
         at = slice(j * CH, (j + 1) * CH)
@@ -202,29 +207,29 @@
             acc[HD:, :] += dot(dots[:, rows], weights)
         return jnp.concatenate([acc[0:HD, :] * SCALE, acc[HD:, :]], axis=0).T.astype(BF)
 
-    def pair_up(j, part):
-        for b in range(16):
-            blk[j, b % 2, b // 2] = part[b * 16:(b + 1) * 16]
-        send(blk.at[j, 1 - c], tpr.at[j], q_ss.at[j], q_rs.at[j], sibling)
-
-    def scatter(j):
-        take(tpr.at[j], q_rs.at[j])
-        tsum[j] = total_of(blk[j, c], tpr[j]).astype(BF)
+    def pair_up(g, parts):
+        for i, part in enumerate(parts):
+            for b in range(16):
+                blk[g, b % 2, b // 2, 16 * i:16 * i + 16] = part[b * 16:(b + 1) * 16]
+        send(blk.at[g, 1 - c], tpr.at[g], q_ss.at[g], q_rs.at[g], sibling)
+
+    def scatter(g):
+        take(tpr.at[g], q_rs.at[g])
+        tsum[g] = total_of(blk[g, c], tpr[g]).astype(BF)
         for k in FAR:
-            send(tsum.at[j, lax.rem(z + k, 8)], t1r.at[j, k], t_ss.at[j, k], t_rs.at[j, k], at_z(k))
-
-    def collect(j):
+            send(tsum.at[g, lax.rem(z + k, 8)], t1r.at[g, k], t_ss.at[g, k], t_rs.at[g, k], at_z(k))
+
+    def collect(g):
         for k in NEAR:
-            take(t1r.at[j, k], t_rs.at[j, k])
-        mine = total_of(tsum[j, z], *[t1r[j, k] for k in range(1, 8)]).astype(BF)
-        rows = slice(16 * j, 16 * j + 16)
-        own[rows, :] = mine
-        og[0, 0, rows] = mine
-        rows = pl.ds(16 * j, 16)
+            take(t1r.at[g, k], t_rs.at[g, k])
+        mine = total_of(tsum[g, z], *[t1r[g, k] for k in range(1, 8)]).astype(BF)
+        own[32 * g:32 * g + 32, :] = mine
+        og[0, 0, 32 * g:32 * g + 32] = mine
+        rows = pl.ds(32 * g, 32)
         for kd, kc in CLUSTER:
-            send(own.at[rows], og.at[kd, kc, rows], a_ss.at[j, kd, kc], a_rs.at[j, kd, kc], at_dc(kd, kc))
+            send(own.at[rows], og.at[kd, kc, rows], a_ss.at[g, kd, kc], a_rs.at[g, kd, kc], at_dc(kd, kc))
         for k in (1, 2, 3):
-            send(own.at[rows], gp.at[k, rows], o_ss.at[j, k], o_rs.at[k], at_y(k))
+            send(own.at[rows], gp.at[k, rows], o_ss.at[g, k], o_rs.at[k], at_y(k))
 
     dkr[...] = backward(4, 4)
     for k in (1, 2, 3):
@@ -245,22 +250,18 @@
     x_s[0] = total_of(pbuf[0, c], prcv[0]).astype(BF)
     send(x_s.at[0], x_r.at[0], x_ss.at[0], x_rs.at[0], at_x(s))
 
-    pair_up(0, backward(0, 5))
+    first = backward(0, 5)
     take(prcv.at[direct], p_rs.at[direct])
     x_s[1] = total_of(pbuf[direct, c], prcv[direct]).astype(BF)
     send(x_s.at[1], x_r.at[1], x_ss.at[1], x_rs.at[1], at_x(-s))
-
-    pair_up(1, backward(1, 5))
+    pair_up(0, (first, backward(1, 5)))
+    third = backward(2, 5)
     scatter(0)
-    pair_up(2, backward(2, 5))
-    scatter(1)
     take(prcv.at[summed], p_rs.at[summed])
     take(x_r.at[0], x_rs.at[0])
     x_s[2] = total_of(pbuf[summed, c], prcv[summed], x_r[0]).astype(BF)
     send(x_s.at[2], x_r.at[2], x_ss.at[2], x_rs.at[2], at_x(s))
-    pair_up(3, backward(3, 5))
-    scatter(2)
-    collect(0)
+    pair_up(1, (third, backward(3, 5)))
 
     def grad_q_block(t):
         rows = slice(t * ROWS, (t + 1) * ROWS)
@@ -273,10 +274,9 @@
 
     grad_q_block(0)
     grad_q_block(1)
-    scatter(3)
-    collect(1)
+    scatter(1)
+    collect(0)
     grad_q_block(2)
-    collect(2)
     grad_q_block(3)
     local.append(move(9, gqr, gqr_h))
     rows = slice(4 * ROWS, 5 * ROWS)
@@ -287,7 +287,7 @@
     for u in range(16):
         gqp[:, u * HD:(u + 1) * HD] = grad_q[u * 64:(u + 1) * 64]
     local.append(move(10, gqp, gqp_h))
-    collect(3)
+    collect(1)
 
     for kd, kc in CLUSTER:
         take(xg.at[kd, kc], xg_rs.at[kd, kc])
@@ -296,32 +296,42 @@
     take(x_r.at[1], x_rs.at[1])
     take(x_r.at[2], x_rs.at[2])
     z_f[...] = total_of(pbuf[3, c], prcv[3], x_r[1], x_r[2])
-    for j in range(4):
+    for g in range(2):
         for kd, kc in CLUSTER:
-            take(og.at[kd, kc, pl.ds(16 * j, 16)], a_rs.at[j, kd, kc])
+            take(og.at[kd, kc, pl.ds(32 * g, 32)], a_rs.at[g, kd, kc])
     z_f[...] += dot(xgt[...], og[...].reshape(512, 256)).reshape(8, 64, 256)
     z_s[...] = z_f[...].astype(BF)
-    for k in FAR:
-        send(z_s.at[lax.rem(z + k, 8)], z_r.at[k], z_ss.at[k], z_rs.at[k], at_z(k))
-
+    zth = lambda k: lax.rem(z + 8 + k, 8)
+    for slot, block, to in ((2, 4, 2 * s), (0, 3, 1), (1, -3, -1), (3, 1, 1), (4, -1, -1)):
+        send(z_s.at[zth(block)], z_r.at[slot], z_ss.at[slot], z_rs.at[slot], at_z(to))
     w_own = wv[pl.ds(pl.multiple_of(h * 1024, 1024), 1024), :]
     for k in (1, 2, 3):
         take(wr.at[k], w_rs.at[k])
         take(gr.at[k], y_rs.at[k])
     gxr[...] = (dot_nt(dkr[...], w_own) + dot_nt(gr[1], wr[1]) + dot_nt(gr[2], wr[2]) + dot_nt(gr[3], wr[3])).astype(BF)
     local.append(move(11, gxr, gxr_h))
+    for slot in range(3):
+        take(z_r.at[slot], z_rs.at[slot])
+    z_m[0] = total_of(z_f[zth(2 * s)], z_r[c], z_r[2]).astype(BF)
+    send(z_m.at[0], z_r.at[5], z_ss.at[5], z_rs.at[5], at_z(2 * s))
+    z_m[1] = total_of(z_f[zth(-2 * s)], z_r[1 - c]).astype(BF)
+    send(z_m.at[1], z_r.at[6], z_ss.at[6], z_rs.at[6], at_z(-2 * s))
+
     for k in (1, 2, 3):
         take(gp.at[k], o_rs.at[k])
     gxp[...] = (dot_nt(own[...], w_own) + dot_nt(gp[1], wr[1]) + dot_nt(gp[2], wr[2]) + dot_nt(gp[3], wr[3])).astype(BF)
     local.append(move(12, gxp, gxp_h))
-    for k in range(1, 8):
-        take(z_r.at[k], z_rs.at[k])
-    gw[...] = total_of(z_f[z], *[z_r[k] for k in range(1, 8)])
-    local.append(move(13, gw, gw_h))
-    for copy in started:
+    for copy in started[:-2]:
         copy.wait_send()
     for copy in local:
         copy.wait()
+    for slot in (3, 4, 5, 6):
+        take(z_r.at[slot], z_rs.at[slot])
+    gw[...] = total_of(z_f[z], z_r[3], z_r[4], z_r[5], z_r[6])
+    last = move(13, gw, gw_h)
+    for copy in started[-2:]:
+        copy.wait_send()
+    last.wait()
 
 
 def layer(length, xp, xr, w, qp, qr, dop, dor):
@@ -337,21 +347,22 @@
     ]
     return pl.pallas_call(
         layer_kernel,
-        in_specs=[pl.BlockSpec(memory_space=pltpu.SMEM)] + [ANY] * 7,
+        in_specs=[ANY] * 8,
         out_specs=[ANY] * 7,
         out_shape=outs,
         scratch_shapes=[
+            pltpu.SMEM((1, 1), jnp.int32),
             bf(64, 4096), bf(256, 4096), bf(4096, 256), bf(64, 2048), bf(256, 2048), bf(64, 2048), bf(256, 2048),
             bf(64, 2048), bf(256, 2048), bf(64, 2048), bf(256, 2048), bf(64, 1024), bf(256, 1024), f32(64, 256),
             bf(4, 16, 16, 256), bf(256, 256), bf(256, 1280), bf(4096, 256), bf(4, 2, 64, 512), bf(4, 2, 64, 512),
             bf(512, 512),            bf(4, 1024, 256),
             bf(5120, 1280), f32(ROWS, 1024), f32(4 * ROWS, CH), bf(5120, HD), bf(5120, HD), bf(HD, 5120), bf(HD, 5120),
             f32(5120, 128), f32(256, 256),
-            bf(4, 2, 8, 16, 256), bf(4, 8, 16, 256), bf(4, 8, 16, 256), bf(4, 8, 16, 256), bf(64, 256),
+            bf(2, 2, 8, 32, 256), bf(2, 8, 32, 256), bf(2, 8, 32, 256), bf(2, 8, 32, 256), bf(64, 256),
             bf(4, 2, 64, 256), bf(4, 64, 256),
             bf(4, 256, 256), bf(256, 256),
-            bf(4, 2, *block), bf(4, *block), bf(3, *block), bf(3, *block), f32(*block), bf(*block), bf(*block),
-            dma((14,)), dma((8,)), dma((8,)), dma((8,)), dma((8,)), dma((4,)), dma((4,)), dma((4, 2)), dma((4, 2)),
+            bf(4, 2, *block), bf(4, *block), bf(3, *block), bf(3, *block), f32(*block), bf(*block), bf(*block), bf(2, 64, 256),
+            dma((15,)), dma((8,)), dma((8,)), dma((8,)), dma((8,)), dma((4,)), dma((4,)), dma((4, 2)), dma((4, 2)),
             dma((4, 8)), dma((4, 8)), dma((4, 4, 2)), dma((4, 4, 2)),
             dma((4,)), dma((4,)), dma((4, 4)), dma((4,)), dma((4,)), dma((4,)), dma((3,)), dma((3,)),
             dma((8,)), dma((8,)), dma((4,)), dma((4,)),

time: 63.3 us -> 64.4 us (1.017)
  Pallas kernels: 61.7 us -> 62.9 us
    pallas_call x1, Pallas kernels: 58.7 us -> 59.8 us  [layer(): pl.pallas_call(layer_kernel, in_specs=[ANY] * 8, out_specs=[ANY] * 7, out...]
where the time goes in v4:
time: 64.4 us; the launch traced here: 64.3 us
  Pallas kernels  62.9 us (98%)
  between operations  1.45 us (2%)
    pallas_call x1, Pallas kernels, layer(): pl.pallas_call(layer_kernel, in_specs=[ANY] * 8, out_specs=[ANY] * 7, out...  59.8 us
    pallas_call x1, Pallas kernels, finish(): pl.pallas_call(finish_kernel, in_specs=[ANY] * n, out_specs=[ANY] * n, ou...  3.06 us

profile of v4, /device:TPU:1, one launch (start us, length us, event | category | flops | bytes accessed | tf_op | source)
XLA Modules:
  0.0 64.3 jit_solution(12198306942180116504)
XLA Ops:
  1.3 59.8 %layer.1 = (bf16[64,2048]{1,0:T(8,128)(2,1)}, bf16[256,2048]{1,0:T(8,128)(2,1)}, bf16[64,2048]{1,0:T(8,128)(2,1)}, bf16[256,2048]{1,0:T(8,128)(2,1)}, bf16[64,10...) custom-call(s32[1,1]{1,0:T(1,128)S(6)} %copy.15.length_h, bf16[64,4096]{1,0:T(8,128)(2,1)} %bitcast.17, ...), custom_call_target="tpu_custom_call" | custom-call | flops 22000001024 | bytes 12582912 | tf_op jit(solution)/shard_map/layer/pallas_call | solution.py:348
  61.1 3.1 %finish.1 = (bf16[64,2048]{1,0:T(8,128)(2,1)}, bf16[256,2048]{1,0:T(8,128)(2,1)}, bf16[64,2048]{1,0:T(8,128)(2,1)}, bf16[256,2048]{1,0:T(8,128)(2,1)}, bf16[64,1...) custom-call(bf16[64,2048]{1,0:T(8,128)(2,1)} %get-tuple-element.21.refs_0_, ...), custom_call_target="tpu_custom_call" | custom-call | tf_op jit(solution)/shard_map/finish/pallas_call | solution.py:397

commit v5 on v4

--- a/solution.py
+++ b/solution.py
@@ -37,9 +37,8 @@
     )
 
 
-FAR = (4, 3, 5, 2, 6, 1, 7)
-NEAR = (1, 7, 2, 6, 3, 5, 4)
 ROWS = 1024
+CHIPS = ((0, 1), (-1, 2), (-2, 3), (-3, 4))
 CLUSTER = ((2, 0), (2, 1), (1, 0), (3, 0), (1, 1), (3, 1), (0, 1))
 
 
@@ -54,8 +53,8 @@
     length_h, xp_h, xr_h, w_h, qp_h, qr_h, dop_h, dor_h,
     op_h, or_h, gqp_h, gqr_h, gxp_h, gxr_h, gw_h,
     length_ref, xp, xr, wv, qp, qr, dop, dor, op, out_r, gqp, gqr, gxp, gxr, gw,
-    kvp, kvr, kt, xrt, xs, xg, xgt, wr,
-    ws, e_ref, e_own, qs, dos, qts, dots, dl, acc,
+    kvp, kvr, kvc, kt, xrt, xs, xg, xgt, wr,
+    ws, qs, dos, qts, dots, dl, acc,
     blk, tpr, tsum, t1r, own, og, gp, gr, dkr,
     pbuf, prcv, x_s, x_r, z_f, z_s, z_r, z_m,
     loc, kv_ss, kv_rs, f_ss, f_rs, w_ss, w_rs, xg_ss, xg_rs, t_ss, t_rs, a_ss, a_rs,
@@ -98,12 +97,11 @@
     loads[0].wait()
     loads[1].wait()
     mine = (dot(xp[...], wv[...]) * fold).astype(BF)
-    for j in range(4):
-        kvp[j, p] = mine[16 * j:16 * j + 16]
+    kvp[z, c] = mine
     pl.semaphore_wait(barrier, len(peers))
     for k in (2, 6, 1, 7):
-        send(kvp.at[:, p], kvp.at[:, p], kv_ss.at[k], kv_rs.at[k], at_z(k))
-    send(kvp.at[:, p], kvp.at[:, p], kv_ss.at[0], kv_rs.at[0], sibling)
+        send(kvp.at[z, c], kvp.at[z, c], kv_ss.at[k], kv_rs.at[k], at_z(k))
+    send(kvp.at[z, c], kvp.at[z, c], kv_ss.at[0], kv_rs.at[0], sibling)
     for k in (2, 1, 3):
         rows = pl.ds(pl.multiple_of(lax.rem(h + k, 4) * 1024, 1024), 1024)
         send(wv.at[rows], wr.at[k], w_ss.at[k], w_rs.at[k], at_y(k))
@@ -134,52 +132,79 @@
         qts[:, rows] = q.T
         dots[:, rows] = do.T
 
+    dl[4 * ROWS:, :] = jnp.zeros((ROWS, 128), F32)
     for t in range(4):
         heads = [slice((t * 4 + u) * HD, (t * 4 + u + 1) * HD) for u in range(4)]
         q = jnp.concatenate([qr[:, head] for head in heads], axis=0)
         do = jnp.concatenate([jnp.where(valid, dor[:, head], jnp.zeros((256, HD), BF)) for head in heads], axis=0)
         keep(t, q, do)
-        e_own[t * ROWS:(t + 1) * ROWS, :] = jnp.where(resp_mask, jnp.exp2(dot(q, kt[0:HD, 1024:])), 0.0)
+        rows = slice(t * ROWS, (t + 1) * ROWS)
+        e = jnp.where(resp_mask, jnp.exp2(dot(q, kt[0:HD, 1024:])), 0.0)
+        ws[rows, 1024:] = e.astype(BF)
+        dl[rows, :] = e[:, :128] + e[:, 128:]
     q = jnp.concatenate([qp[:, u * HD:(u + 1) * HD] for u in range(16)], axis=0)
     do = jnp.concatenate([dop[:, u * HD:(u + 1) * HD] for u in range(16)], axis=0)
     keep(4, q, do)
-    came = lambda k: kvp.at[:, lax.rem(z + 16 - k, 8) * 2 + c]
+    came = lambda k: kvp.at[lax.rem(z + 16 - k, 8), c]
+    zth = lambda k: lax.rem(z + 8 + k, 8)
+
+    def across(k):
+        send(came(k), came(k), f_ss.at[k], f_rs.at[k], sibling)
+
+    def crossed(k):
+        take(kvp.at[zth(-k), 1 - c], f_rs.at[k])
+
+    def scores(j):
+        near, far = (zth(k) for k in CHIPS[j])
+        at = slice(j * CH, (j + 1) * CH)
+        kvc[j] = jnp.concatenate([kvp[near].reshape(128, 256), kvp[far].reshape(128, 256)], axis=0)
+        kt[:, at] = kvc[j].T
+        for t in range(5):
+            rows = slice(t * ROWS, (t + 1) * ROWS)
+            e = jnp.exp2(dot(qs[rows, :], kt[0:HD, at]))
+            if t == 4:
+                place = jnp.where(col < 128, near * 128, far * 128) + (col & 127)
+                e = jnp.where(place <= (row & 63) + offset, e, 0.0)
+            ws[rows, at] = e.astype(BF)
+            dl[rows, :] += e[:, :128] + e[:, 128:]
+
     for k, to in ((2, 1), (6, -1)):
         take(came(k), kv_rs.at[k])
         send(came(k), came(k), kv_ss.at[4 - to], kv_rs.at[4 - to], at_z(to))
     send(came(2 * s), came(2 * s), kv_ss.at[4], kv_rs.at[4], at_z(2 * s))
-    for k in (2, 6, 1, 7, 3, 5, 4):
-        if k not in (2, 6):
-            take(came(k), kv_rs.at[k])
-        send(came(k), came(k), f_ss.at[k], f_rs.at[k], sibling)
-    take(kvp.at[:, z * 2 + 1 - c], kv_rs.at[0])
-    for k in NEAR:
-        take(kvp.at[:, lax.rem(z + 8 - k, 8) * 2 + 1 - c], f_rs.at[k])
-    for j in range(4):
-        kt[:, j * CH:(j + 1) * CH] = kvp[j].reshape(CH, 2 * HD).T
+    for k in (7, 1):
+        take(came(k), kv_rs.at[k])
+        across(k)
+    across(6)
+    across(2)
+    take(kvp.at[z, 1 - c], kv_rs.at[0])
+    crossed(7)
+    scores(0)
+    crossed(1)
+    crossed(6)
+    scores(1)
+    for k in (5, 3, 4):
+        take(came(k), kv_rs.at[k])
+        across(k)
+    crossed(2)
+    crossed(5)
+    scores(2)
+    crossed(3)
+    crossed(4)
+    scores(3)
 
     def kv_of(j):
-        return kvr[...] if j == 4 else kvp[j].reshape(CH, 2 * HD)
+        return kvr[...] if j == 4 else kvc[j]
 
     def forward(t):
         rows = slice(t * ROWS, (t + 1) * ROWS)
-        q, do = qs[rows, :], dos[rows, :]
-        total = jnp.zeros((ROWS, 128), F32)
-        for j in range(4):
-            e = jnp.exp2(dot(q, kt[0:HD, j * CH:(j + 1) * CH]))
-            if t == 4:
-                allowed = (col >> 4) * 64 + (col & 15) + 16 * j <= (row & 63) + offset
-                e = jnp.where(allowed, e, 0.0)
-            e_ref[:, j * CH:(j + 1) * CH] = e
-            total = total + e[:, :128] + e[:, 128:]
-        if t < 4:
-            total = total + e_own[rows, :128] + e_own[rows, 128:]
-        inverse = 1.0 / jnp.sum(total, axis=1, keepdims=True)
+        do = dos[rows, :]
+        inverse = 1.0 / jnp.sum(dl[rows, :], axis=1, keepdims=True)
         out = jnp.zeros((ROWS, HD), F32)
         for j in range(4 if t == 4 else 5):
-            e = e_own[rows, :] if j == 4 else e_ref[:, j * CH:(j + 1) * CH]
-            weights = (e * inverse).astype(BF)
-            ws[rows, j * CH:(j + 1) * CH] = weights
+            at = slice(j * CH, (j + 1) * CH)
+            weights = (ws[rows, at].astype(F32) * inverse).astype(BF)
+            ws[rows, at] = weights
             out = out + dot(weights, kv_of(j)[:, HD:])
         out = out.astype(BF)
         delta = jnp.sum(do.astype(F32) * out.astype(F32), axis=1, keepdims=True)
@@ -207,29 +232,28 @@
             acc[HD:, :] += dot(dots[:, rows], weights)
         return jnp.concatenate([acc[0:HD, :] * SCALE, acc[HD:, :]], axis=0).T.astype(BF)
 
-    def pair_up(g, parts):
-        for i, part in enumerate(parts):
-            for b in range(16):
-                blk[g, b % 2, b // 2, 16 * i:16 * i + 16] = part[b * 16:(b + 1) * 16]
-        send(blk.at[g, 1 - c], tpr.at[g], q_ss.at[g], q_rs.at[g], sibling)
-
-    def scatter(g):
-        take(tpr.at[g], q_rs.at[g])
-        tsum[g] = total_of(blk[g, c], tpr[g]).astype(BF)
-        for k in FAR:
-            send(tsum.at[g, lax.rem(z + k, 8)], t1r.at[g, k], t_ss.at[g, k], t_rs.at[g, k], at_z(k))
-
-    def collect(g):
-        for k in NEAR:
-            take(t1r.at[g, k], t_rs.at[g, k])
-        mine = total_of(tsum[g, z], *[t1r[g, k] for k in range(1, 8)]).astype(BF)
-        own[32 * g:32 * g + 32, :] = mine
-        og[0, 0, 32 * g:32 * g + 32] = mine
-        rows = pl.ds(32 * g, 32)
+    def pair_up(j, part):
+        for i in range(4):
+            blk[j, i % 2, i // 2] = part[64 * i:64 * i + 64]
+        send(blk.at[j, 1 - c], tpr.at[j], q_ss.at[j], q_rs.at[j], sibling)
+
+    def scatter(j):
+        take(tpr.at[j], q_rs.at[j])
+        tsum[j] = total_of(blk[j, c], tpr[j]).astype(BF)
+        for i, k in enumerate(CHIPS[j]):
+            if k != 0:
+                send(tsum.at[j, i], t1r.at[k % 8], t_ss.at[k % 8], t_rs.at[k % 8], at_z(k))
+
+    def collect():
+        for k in range(1, 8):
+            take(t1r.at[k], t_rs.at[k])
+        mine = total_of(tsum[0, 0], *[t1r[k] for k in range(1, 8)]).astype(BF)
+        own[...] = mine
+        og[0, 0] = mine
         for kd, kc in CLUSTER:
-            send(own.at[rows], og.at[kd, kc, rows], a_ss.at[g, kd, kc], a_rs.at[g, kd, kc], at_dc(kd, kc))
+            send(own, og.at[kd, kc], a_ss.at[kd, kc], a_rs.at[kd, kc], at_dc(kd, kc))
         for k in (1, 2, 3):
-            send(own.at[rows], gp.at[k, rows], o_ss.at[g, k], o_rs.at[k], at_y(k))
+            send(own, gp.at[k], o_ss.at[k], o_rs.at[k], at_y(k))
 
     dkr[...] = backward(4, 4)
     for k in (1, 2, 3):
@@ -250,18 +274,20 @@
     x_s[0] = total_of(pbuf[0, c], prcv[0]).astype(BF)
     send(x_s.at[0], x_r.at[0], x_ss.at[0], x_rs.at[0], at_x(s))
 
-    first = backward(0, 5)
+    pair_up(3, backward(3, 5))
     take(prcv.at[direct], p_rs.at[direct])
     x_s[1] = total_of(pbuf[direct, c], prcv[direct]).astype(BF)
     send(x_s.at[1], x_r.at[1], x_ss.at[1], x_rs.at[1], at_x(-s))
-    pair_up(0, (first, backward(1, 5)))
-    third = backward(2, 5)
-    scatter(0)
+    pair_up(2, backward(2, 5))
+    scatter(3)
+    pair_up(1, backward(1, 5))
+    scatter(2)
     take(prcv.at[summed], p_rs.at[summed])
     take(x_r.at[0], x_rs.at[0])
     x_s[2] = total_of(pbuf[summed, c], prcv[summed], x_r[0]).astype(BF)
     send(x_s.at[2], x_r.at[2], x_ss.at[2], x_rs.at[2], at_x(s))
-    pair_up(1, (third, backward(3, 5)))
+    pair_up(0, backward(0, 5))
+    scatter(1)
 
     def grad_q_block(t):
         rows = slice(t * ROWS, (t + 1) * ROWS)
@@ -274,8 +300,7 @@
 
     grad_q_block(0)
     grad_q_block(1)
-    scatter(1)
-    collect(0)
+    scatter(0)
     grad_q_block(2)
     grad_q_block(3)
     local.append(move(9, gqr, gqr_h))
@@ -287,7 +312,7 @@
     for u in range(16):
         gqp[:, u * HD:(u + 1) * HD] = grad_q[u * 64:(u + 1) * 64]
     local.append(move(10, gqp, gqp_h))
-    collect(1)
+    collect()
 
     for kd, kc in CLUSTER:
         take(xg.at[kd, kc], xg_rs.at[kd, kc])
@@ -296,12 +321,10 @@
     take(x_r.at[1], x_rs.at[1])
     take(x_r.at[2], x_rs.at[2])
     z_f[...] = total_of(pbuf[3, c], prcv[3], x_r[1], x_r[2])
-    for g in range(2):
-        for kd, kc in CLUSTER:
-            take(og.at[kd, kc, pl.ds(32 * g, 32)], a_rs.at[g, kd, kc])
+    for kd, kc in CLUSTER:
+        take(og.at[kd, kc], a_rs.at[kd, kc])
     z_f[...] += dot(xgt[...], og[...].reshape(512, 256)).reshape(8, 64, 256)
     z_s[...] = z_f[...].astype(BF)
-    zth = lambda k: lax.rem(z + 8 + k, 8)
     for slot, block, to in ((2, 4, 2 * s), (0, 3, 1), (1, -3, -1), (3, 1, 1), (4, -1, -1)):
         send(z_s.at[zth(block)], z_r.at[slot], z_ss.at[slot], z_rs.at[slot], at_z(to))
     w_own = wv[pl.ds(pl.multiple_of(h * 1024, 1024), 1024), :]
@@ -354,17 +377,17 @@
             pltpu.SMEM((1, 1), jnp.int32),
             bf(64, 4096), bf(256, 4096), bf(4096, 256), bf(64, 2048), bf(256, 2048), bf(64, 2048), bf(256, 2048),
             bf(64, 2048), bf(256, 2048), bf(64, 2048), bf(256, 2048), bf(64, 1024), bf(256, 1024), f32(64, 256),
-            bf(4, 16, 16, 256), bf(256, 256), bf(256, 1280), bf(4096, 256), bf(4, 2, 64, 512), bf(4, 2, 64, 512),
+            bf(8, 2, 64, 256), bf(256, 256), bf(4, 256, 256), bf(256, 1280), bf(4096, 256), bf(4, 2, 64, 512), bf(4, 2, 64, 512),
             bf(512, 512),            bf(4, 1024, 256),
-            bf(5120, 1280), f32(ROWS, 1024), f32(4 * ROWS, CH), bf(5120, HD), bf(5120, HD), bf(HD, 5120), bf(HD, 5120),
+            bf(5120, 1280), bf(5120, HD), bf(5120, HD), bf(HD, 5120), bf(HD, 5120),
             f32(5120, 128), f32(256, 256),
-            bf(2, 2, 8, 32, 256), bf(2, 8, 32, 256), bf(2, 8, 32, 256), bf(2, 8, 32, 256), bf(64, 256),
+            bf(4, 2, 2, 64, 256), bf(4, 2, 64, 256), bf(4, 2, 64, 256), bf(8, 64, 256), bf(64, 256),
             bf(4, 2, 64, 256), bf(4, 64, 256),
             bf(4, 256, 256), bf(256, 256),
             bf(4, 2, *block), bf(4, *block), bf(3, *block), bf(3, *block), f32(*block), bf(*block), bf(*block), bf(2, 64, 256),
             dma((15,)), dma((8,)), dma((8,)), dma((8,)), dma((8,)), dma((4,)), dma((4,)), dma((4, 2)), dma((4, 2)),
-            dma((4, 8)), dma((4, 8)), dma((4, 4, 2)), dma((4, 4, 2)),
-            dma((4,)), dma((4,)), dma((4, 4)), dma((4,)), dma((4,)), dma((4,)), dma((3,)), dma((3,)),
+            dma((8,)), dma((8,)), dma((4, 2)), dma((4, 2)),
+            dma((4,)), dma((4,)), dma((4,)), dma((4,)), dma((4,)), dma((4,)), dma((3,)), dma((3,)),
             dma((8,)), dma((8,)), dma((4,)), dma((4,)),
         ],
         compiler_params=pltpu.CompilerParams(

time: 64.4 us -> 62.4 us (0.969)
  Pallas kernels: 62.9 us -> 60.8 us
    pallas_call x1, Pallas kernels: 59.8 us -> 57.7 us  [layer(): pl.pallas_call(layer_kernel, in_specs=[ANY] * 8, out_specs=[ANY] * 7, out...]
where the time goes in v5:
time: 62.4 us; the launch traced here: 62.3 us
  Pallas kernels  60.8 us (97%)
  between operations  1.45 us (2%)
    pallas_call x1, Pallas kernels, layer(): pl.pallas_call(layer_kernel, in_specs=[ANY] * 8, out_specs=[ANY] * 7, out...  57.7 us
    pallas_call x1, Pallas kernels, finish(): pl.pallas_call(finish_kernel, in_specs=[ANY] * n, out_specs=[ANY] * n, ou...  3.06 us

profile of v5, /device:TPU:1, one launch (start us, length us, event | category | flops | bytes accessed | tf_op | source)
XLA Modules:
  0.0 62.3 jit_solution(3472384346289782357)
XLA Ops:
  1.3 57.7 %layer.1 = (bf16[64,2048]{1,0:T(8,128)(2,1)}, bf16[256,2048]{1,0:T(8,128)(2,1)}, bf16[64,2048]{1,0:T(8,128)(2,1)}, bf16[256,2048]{1,0:T(8,128)(2,1)}, bf16[64,10...) custom-call(s32[1,1]{1,0:T(1,128)S(6)} %copy.15.length_h, bf16[64,4096]{1,0:T(8,128)(2,1)} %bitcast.17, ...), custom_call_target="tpu_custom_call" | custom-call | flops 22000001024 | bytes 12582912 | tf_op jit(solution)/shard_map/layer/pallas_call | solution.py:371
  59.0 3.1 %finish.1 = (bf16[64,2048]{1,0:T(8,128)(2,1)}, bf16[256,2048]{1,0:T(8,128)(2,1)}, bf16[64,2048]{1,0:T(8,128)(2,1)}, bf16[256,2048]{1,0:T(8,128)(2,1)}, bf16[64,1...) custom-call(bf16[64,2048]{1,0:T(8,128)(2,1)} %get-tuple-element.21.refs_0_, ...), custom_call_target="tpu_custom_call" | custom-call | tf_op jit(solution)/shard_map/finish/pallas_call | solution.py:420

commit v6 on v5

--- a/solution.py
+++ b/solution.py
@@ -55,10 +55,10 @@
     length_ref, xp, xr, wv, qp, qr, dop, dor, op, out_r, gqp, gqr, gxp, gxr, gw,
     kvp, kvr, kvc, kt, xrt, xs, xg, xgt, wr,
     ws, qs, dos, qts, dots, dl, acc,
-    blk, tpr, tsum, t1r, own, og, gp, gr, dkr,
+    blk, tpr, tsum, t1r, tnear, own, og, gp, gr, dkr,
     pbuf, prcv, x_s, x_r, z_f, z_s, z_r, z_m,
     loc, kv_ss, kv_rs, f_ss, f_rs, w_ss, w_rs, xg_ss, xg_rs, t_ss, t_rs, a_ss, a_rs,
-    y_ss, y_rs, o_ss, o_rs, p_ss, p_rs, x_ss, x_rs, z_ss, z_rs, q_ss, q_rs,
+    y_ss, y_rs, o_ss, o_rs, p_ss, p_rs, x_ss, x_rs, z_ss, z_rs, q_ss, q_rs, n_ss, n_rs,
 ):
     d, h = lax.axis_index("dp"), lax.axis_index("head")
     p = lax.axis_index("pool")
@@ -69,6 +69,7 @@
     at_x = lambda k: (lax.rem(d + 4 + k, 4), p, h)
     at_y = lambda k: (d, p, lax.rem(h + k, 4))
     sibling = (d, z * 2 + 1 - c, h)
+    diagonal = lambda k: (d, lax.rem(z + 8 + k, 8) * 2 + 1 - c, h)
     started, local = [], []
 
     def send(*args):
@@ -89,6 +90,7 @@
         ((xp_h, xp), (w_h, wv), (xr_h, xr), (qr_h, qr), (dor_h, dor), (qp_h, qp), (dop_h, dop), (length_h, length_ref)))]
     barrier = pltpu.get_barrier_semaphore()
     peers = [at_z(k) for k in range(1, 8)] + [at_dc(*k) for k in CLUSTER] + [at_y(k) for k in (1, 2, 3)]
+    peers += [diagonal(1), diagonal(-1)]
     for peer in peers:
         pl.semaphore_signal(barrier, inc=1, device_id=peer, device_id_type=MESH)
 
@@ -108,15 +110,6 @@
     loads[2].wait()
     kvr[...] = (dot(xr[...], wv[...]) * fold).astype(BF)
     kt[:, 1024:] = kvr[...].T
-    for q in range(4):
-        for half in range(2):
-            starts = [q * 1024 + b * 128 + half * 64 for b in range(8)]
-            xs[q, half] = jnp.concatenate([xp[:, i:i + 64] for i in starts], axis=1)
-    xg[0, 0] = xs[d, c]
-    for kd, kc in CLUSTER:
-        send(xs.at[lax.rem(d + kd, 4), lax.rem(c + kc, 2)], xg.at[kd, kc], xg_ss.at[kd, kc], xg_rs.at[kd, kc], at_dc(kd, kc))
-    for i in range(16):
-        xrt[i * 256:(i + 1) * 256, :] = xr[:, i * 256:(i + 1) * 256].T
     for copy in loads[3:]:
         copy.wait()
     length, offset = length_ref[0, 0], p * 64
@@ -132,19 +125,6 @@
         qts[:, rows] = q.T
         dots[:, rows] = do.T
 
-    dl[4 * ROWS:, :] = jnp.zeros((ROWS, 128), F32)
-    for t in range(4):
-        heads = [slice((t * 4 + u) * HD, (t * 4 + u + 1) * HD) for u in range(4)]
-        q = jnp.concatenate([qr[:, head] for head in heads], axis=0)
-        do = jnp.concatenate([jnp.where(valid, dor[:, head], jnp.zeros((256, HD), BF)) for head in heads], axis=0)
-        keep(t, q, do)
-        rows = slice(t * ROWS, (t + 1) * ROWS)
-        e = jnp.where(resp_mask, jnp.exp2(dot(q, kt[0:HD, 1024:])), 0.0)
-        ws[rows, 1024:] = e.astype(BF)
-        dl[rows, :] = e[:, :128] + e[:, 128:]
-    q = jnp.concatenate([qp[:, u * HD:(u + 1) * HD] for u in range(16)], axis=0)
-    do = jnp.concatenate([dop[:, u * HD:(u + 1) * HD] for u in range(16)], axis=0)
-    keep(4, q, do)
     came = lambda k: kvp.at[lax.rem(z + 16 - k, 8), c]
     zth = lambda k: lax.rem(z + 8 + k, 8)
 
@@ -168,6 +148,18 @@
             ws[rows, at] = e.astype(BF)
             dl[rows, :] += e[:, :128] + e[:, 128:]
 
+    def prepare(t):
+        heads = [slice((t * 4 + u) * HD, (t * 4 + u + 1) * HD) for u in range(4)]
+        q = jnp.concatenate([qr[:, head] for head in heads], axis=0)
+        do = jnp.concatenate([jnp.where(valid, dor[:, head], jnp.zeros((256, HD), BF)) for head in heads], axis=0)
+        keep(t, q, do)
+        rows = slice(t * ROWS, (t + 1) * ROWS)
+        e = jnp.where(resp_mask, jnp.exp2(dot(q, kt[0:HD, 1024:])), 0.0)
+        ws[rows, 1024:] = e.astype(BF)
+        dl[rows, :] = e[:, :128] + e[:, 128:]
+
+    prepare(0)
+    prepare(1)
     for k, to in ((2, 1), (6, -1)):
         take(came(k), kv_rs.at[k])
         send(came(k), came(k), kv_ss.at[4 - to], kv_rs.at[4 - to], at_z(to))
@@ -177,6 +169,12 @@
         across(k)
     across(6)
     across(2)
+    prepare(2)
+    prepare(3)
+    dl[4 * ROWS:, :] = jnp.zeros((ROWS, 128), F32)
+    q = jnp.concatenate([qp[:, u * HD:(u + 1) * HD] for u in range(16)], axis=0)
+    do = jnp.concatenate([dop[:, u * HD:(u + 1) * HD] for u in range(16)], axis=0)
+    keep(4, q, do)
     take(kvp.at[z, 1 - c], kv_rs.at[0])
     crossed(7)
     scores(0)
@@ -186,6 +184,15 @@
     for k in (5, 3, 4):
         take(came(k), kv_rs.at[k])
         across(k)
+    for q in range(4):
+        for half in range(2):
+            starts = [q * 1024 + b * 128 + half * 64 for b in range(8)]
+            xs[q, half] = jnp.concatenate([xp[:, i:i + 64] for i in starts], axis=1)
+    xg[0, 0] = xs[d, c]
+    for kd, kc in CLUSTER:
+        send(xs.at[lax.rem(d + kd, 4), lax.rem(c + kc, 2)], xg.at[kd, kc], xg_ss.at[kd, kc], xg_rs.at[kd, kc], at_dc(kd, kc))
+    for i in range(16):
+        xrt[i * 256:(i + 1) * 256, :] = xr[:, i * 256:(i + 1) * 256].T
     crossed(2)
     crossed(5)
     scores(2)
@@ -241,13 +248,21 @@
         take(tpr.at[j], q_rs.at[j])
         tsum[j] = total_of(blk[j, c], tpr[j]).astype(BF)
         for i, k in enumerate(CHIPS[j]):
-            if k != 0:
-                send(tsum.at[j, i], t1r.at[k % 8], t_ss.at[k % 8], t_rs.at[k % 8], at_z(k))
+            send(tsum.at[j, i], t1r.at[k % 8], t_ss.at[k % 8], t_rs.at[k % 8], at_z(k))
+
+    def spread(part):
+        for i in range(4):
+            blk[0, i % 2, i // 2] = part[64 * i:64 * i + 64]
+        send(blk.at[0, c, 1], tnear.at[0], n_ss.at[0], n_rs.at[0], at_z(1))
+        send(blk.at[0, 1 - c, 1], tnear.at[1], n_ss.at[1], n_rs.at[1], diagonal(1))
+        send(blk.at[0, 1 - c, 0], tnear.at[2], n_ss.at[2], n_rs.at[2], sibling)
 
     def collect():
-        for k in range(1, 8):
+        for k in range(2, 8):
             take(t1r.at[k], t_rs.at[k])
-        mine = total_of(tsum[0, 0], *[t1r[k] for k in range(1, 8)]).astype(BF)
+        for k in range(3):
+            take(tnear.at[k], n_rs.at[k])
+        mine = total_of(blk[0, c, 0], *[tnear[k] for k in range(3)], *[t1r[k] for k in range(2, 8)]).astype(BF)
         own[...] = mine
         og[0, 0] = mine
         for kd, kc in CLUSTER:
@@ -286,7 +301,7 @@
     take(x_r.at[0], x_rs.at[0])
     x_s[2] = total_of(pbuf[summed, c], prcv[summed], x_r[0]).astype(BF)
     send(x_s.at[2], x_r.at[2], x_ss.at[2], x_rs.at[2], at_x(s))
-    pair_up(0, backward(0, 5))
+    spread(backward(0, 5))
     scatter(1)
 
     def grad_q_block(t):
@@ -300,7 +315,6 @@
 
     grad_q_block(0)
     grad_q_block(1)
-    scatter(0)
     grad_q_block(2)
     grad_q_block(3)
     local.append(move(9, gqr, gqr_h))
@@ -381,14 +395,14 @@
             bf(512, 512),            bf(4, 1024, 256),
             bf(5120, 1280), bf(5120, HD), bf(5120, HD), bf(HD, 5120), bf(HD, 5120),
             f32(5120, 128), f32(256, 256),
-            bf(4, 2, 2, 64, 256), bf(4, 2, 64, 256), bf(4, 2, 64, 256), bf(8, 64, 256), bf(64, 256),
+            bf(4, 2, 2, 64, 256), bf(4, 2, 64, 256), bf(4, 2, 64, 256), bf(8, 64, 256), bf(3, 64, 256), bf(64, 256),
             bf(4, 2, 64, 256), bf(4, 64, 256),
             bf(4, 256, 256), bf(256, 256),
             bf(4, 2, *block), bf(4, *block), bf(3, *block), bf(3, *block), f32(*block), bf(*block), bf(*block), bf(2, 64, 256),
             dma((15,)), dma((8,)), dma((8,)), dma((8,)), dma((8,)), dma((4,)), dma((4,)), dma((4, 2)), dma((4, 2)),
             dma((8,)), dma((8,)), dma((4, 2)), dma((4, 2)),
             dma((4,)), dma((4,)), dma((4,)), dma((4,)), dma((4,)), dma((4,)), dma((3,)), dma((3,)),
-            dma((8,)), dma((8,)), dma((4,)), dma((4,)),
+            dma((8,)), dma((8,)), dma((4,)), dma((4,)), dma((3,)), dma((3,)),
         ],
         compiler_params=pltpu.CompilerParams(
             collective_id=0, has_side_effects=True, vmem_limit_bytes=60 << 20

time: 62.4 us -> 60.8 us (0.974); the launches traced: 62.3 us -> 59.9 us
  Pallas kernels: 60.8 us -> 58.4 us
    pallas_call x1, Pallas kernels: 57.7 us -> 55.4 us  [layer(): pl.pallas_call(layer_kernel, in_specs=[ANY] * 8, out_specs=[ANY] * 7, out...]
where the time goes in v6:
time: 60.8 us; the launch traced here: 59.9 us
  Pallas kernels  58.4 us (96%)
  between operations  1.45 us (2%)
    pallas_call x1, Pallas kernels, layer(): pl.pallas_call(layer_kernel, in_specs=[ANY] * 8, out_specs=[ANY] * 7, out...  55.4 us
    pallas_call x1, Pallas kernels, finish(): pl.pallas_call(finish_kernel, in_specs=[ANY] * n, out_specs=[ANY] * n, ou...  3.06 us

profile of v6, /device:TPU:1, one launch (start us, length us, event | category | flops | bytes accessed | tf_op | source)
XLA Modules:
  0.0 59.9 jit_solution(16238533789154270695)
XLA Ops:
  1.3 55.4 %layer.1 = (bf16[64,2048]{1,0:T(8,128)(2,1)}, bf16[256,2048]{1,0:T(8,128)(2,1)}, bf16[64,2048]{1,0:T(8,128)(2,1)}, bf16[256,2048]{1,0:T(8,128)(2,1)}, bf16[64,10...) custom-call(s32[1,1]{1,0:T(1,128)S(6)} %copy.15.length_h, bf16[64,4096]{1,0:T(8,128)(2,1)} %bitcast.17, ...), custom_call_target="tpu_custom_call" | custom-call | flops 22000001024 | bytes 12582912 | tf_op jit(solution)/shard_map/layer/pallas_call | solution.py:385
  56.7 3.1 %finish.1 = (bf16[64,2048]{1,0:T(8,128)(2,1)}, bf16[256,2048]{1,0:T(8,128)(2,1)}, bf16[64,2048]{1,0:T(8,128)(2,1)}, bf16[256,2048]{1,0:T(8,128)(2,1)}, bf16[64,1...) custom-call(bf16[64,2048]{1,0:T(8,128)(2,1)} %get-tuple-element.21.refs_0_, ...), custom_call_target="tpu_custom_call" | custom-call | tf_op jit(solution)/shard_map/finish/pallas_call | solution.py:434

commit v7 on v6

--- a/solution.py
+++ b/solution.py
@@ -90,7 +90,7 @@
         ((xp_h, xp), (w_h, wv), (xr_h, xr), (qr_h, qr), (dor_h, dor), (qp_h, qp), (dop_h, dop), (length_h, length_ref)))]
     barrier = pltpu.get_barrier_semaphore()
     peers = [at_z(k) for k in range(1, 8)] + [at_dc(*k) for k in CLUSTER] + [at_y(k) for k in (1, 2, 3)]
-    peers += [diagonal(1), diagonal(-1)]
+    peers += [diagonal(k) for k in (1, -1, 2, -2)]
     for peer in peers:
         pl.semaphore_signal(barrier, inc=1, device_id=peer, device_id_type=MESH)
 
@@ -250,19 +250,24 @@
         for i, k in enumerate(CHIPS[j]):
             send(tsum.at[j, i], t1r.at[k % 8], t_ss.at[k % 8], t_rs.at[k % 8], at_z(k))
 
-    def spread(part):
+    def spread(j, part):
         for i in range(4):
-            blk[0, i % 2, i // 2] = part[64 * i:64 * i + 64]
-        send(blk.at[0, c, 1], tnear.at[0], n_ss.at[0], n_rs.at[0], at_z(1))
-        send(blk.at[0, 1 - c, 1], tnear.at[1], n_ss.at[1], n_rs.at[1], diagonal(1))
-        send(blk.at[0, 1 - c, 0], tnear.at[2], n_ss.at[2], n_rs.at[2], sibling)
+            blk[j, i % 2, i // 2] = part[64 * i:64 * i + 64]
+        for i, k in enumerate(CHIPS[j]):
+            if k != 0:
+                send(blk.at[j, c, i], tnear.at[j, i, 0], n_ss.at[j, i, 0], n_rs.at[j, i, 0], at_z(k))
+            to = diagonal(k) if k != 0 else sibling
+            send(blk.at[j, 1 - c, i], tnear.at[j, i, 1], n_ss.at[j, i, 1], n_rs.at[j, i, 1], to)
 
     def collect():
-        for k in range(2, 8):
+        spots = [(j, i, half) for j in (1, 0) for i in range(2) for half in range(2) if (j, i, half) != (0, 0, 0)]
+        for k in range(3, 7):
             take(t1r.at[k], t_rs.at[k])
-        for k in range(3):
-            take(tnear.at[k], n_rs.at[k])
-        mine = total_of(blk[0, c, 0], *[tnear[k] for k in range(3)], *[t1r[k] for k in range(2, 8)]).astype(BF)
+        for spot in spots:
+            take(tnear.at[spot], n_rs.at[spot])
+        mine = total_of(
+            blk[0, c, 0], *[tnear[spot] for spot in spots], *[t1r[k] for k in range(3, 7)]
+        ).astype(BF)
         own[...] = mine
         og[0, 0] = mine
         for kd, kc in CLUSTER:
@@ -295,14 +300,13 @@
     send(x_s.at[1], x_r.at[1], x_ss.at[1], x_rs.at[1], at_x(-s))
     pair_up(2, backward(2, 5))
     scatter(3)
-    pair_up(1, backward(1, 5))
+    spread(1, backward(1, 5))
     scatter(2)
     take(prcv.at[summed], p_rs.at[summed])
     take(x_r.at[0], x_rs.at[0])
     x_s[2] = total_of(pbuf[summed, c], prcv[summed], x_r[0]).astype(BF)
     send(x_s.at[2], x_r.at[2], x_ss.at[2], x_rs.at[2], at_x(s))
-    spread(backward(0, 5))
-    scatter(1)
+    spread(0, backward(0, 5))
 
     def grad_q_block(t):
         rows = slice(t * ROWS, (t + 1) * ROWS)
@@ -316,6 +320,7 @@
     grad_q_block(0)
     grad_q_block(1)
     grad_q_block(2)
+    collect()
     grad_q_block(3)
     local.append(move(9, gqr, gqr_h))
     rows = slice(4 * ROWS, 5 * ROWS)
@@ -326,7 +331,6 @@
     for u in range(16):
         gqp[:, u * HD:(u + 1) * HD] = grad_q[u * 64:(u + 1) * 64]
     local.append(move(10, gqp, gqp_h))
-    collect()
 
     for kd, kc in CLUSTER:
         take(xg.at[kd, kc], xg_rs.at[kd, kc])
@@ -395,14 +399,14 @@
             bf(512, 512),            bf(4, 1024, 256),
             bf(5120, 1280), bf(5120, HD), bf(5120, HD), bf(HD, 5120), bf(HD, 5120),
             f32(5120, 128), f32(256, 256),
-            bf(4, 2, 2, 64, 256), bf(4, 2, 64, 256), bf(4, 2, 64, 256), bf(8, 64, 256), bf(3, 64, 256), bf(64, 256),
+            bf(4, 2, 2, 64, 256), bf(4, 2, 64, 256), bf(4, 2, 64, 256), bf(8, 64, 256), bf(2, 2, 2, 64, 256), bf(64, 256),
             bf(4, 2, 64, 256), bf(4, 64, 256),
             bf(4, 256, 256), bf(256, 256),
             bf(4, 2, *block), bf(4, *block), bf(3, *block), bf(3, *block), f32(*block), bf(*block), bf(*block), bf(2, 64, 256),
             dma((15,)), dma((8,)), dma((8,)), dma((8,)), dma((8,)), dma((4,)), dma((4,)), dma((4, 2)), dma((4, 2)),
             dma((8,)), dma((8,)), dma((4, 2)), dma((4, 2)),
             dma((4,)), dma((4,)), dma((4,)), dma((4,)), dma((4,)), dma((4,)), dma((3,)), dma((3,)),
-            dma((8,)), dma((8,)), dma((4,)), dma((4,)), dma((3,)), dma((3,)),
+            dma((8,)), dma((8,)), dma((4,)), dma((4,)), dma((2, 2, 2)), dma((2, 2, 2)),
         ],
         compiler_params=pltpu.CompilerParams(
             collective_id=0, has_side_effects=True, vmem_limit_bytes=60 << 20

time: 60.8 us -> 62.9 us (1.035); the launches traced: 59.9 us -> 62.8 us
  Pallas kernels: 58.4 us -> 61.4 us
    pallas_call x1, Pallas kernels: 55.4 us -> 58.3 us  [layer(): pl.pallas_call(layer_kernel, in_specs=[ANY] * 8, out_specs=[ANY] * 7, out...]
where the time goes in v7:
time: 62.9 us; the launch traced here: 62.8 us
  Pallas kernels  61.4 us (98%)
  between operations  1.45 us (2%)
    pallas_call x1, Pallas kernels, layer(): pl.pallas_call(layer_kernel, in_specs=[ANY] * 8, out_specs=[ANY] * 7, out...  58.3 us
    pallas_call x1, Pallas kernels, finish(): pl.pallas_call(finish_kernel, in_specs=[ANY] * n, out_specs=[ANY] * n, ou...  3.06 us

profile of v7, /device:TPU:1, one launch (start us, length us, event | category | flops | bytes accessed | tf_op | source)
XLA Modules:
  0.0 62.8 jit_solution(5295853106173247884)
XLA Ops:
  1.3 58.3 %layer.1 = (bf16[64,2048]{1,0:T(8,128)(2,1)}, bf16[256,2048]{1,0:T(8,128)(2,1)}, bf16[64,2048]{1,0:T(8,128)(2,1)}, bf16[256,2048]{1,0:T(8,128)(2,1)}, bf16[64,10...) custom-call(s32[1,1]{1,0:T(1,128)S(6)} %copy.15.length_h, bf16[64,4096]{1,0:T(8,128)(2,1)} %bitcast.17, ...), custom_call_target="tpu_custom_call" | custom-call | flops 22000001024 | bytes 12582912 | tf_op jit(solution)/shard_map/layer/pallas_call | solution.py:389
  59.6 3.1 %finish.1 = (bf16[64,2048]{1,0:T(8,128)(2,1)}, bf16[256,2048]{1,0:T(8,128)(2,1)}, bf16[64,2048]{1,0:T(8,128)(2,1)}, bf16[256,2048]{1,0:T(8,128)(2,1)}, bf16[64,1...) custom-call(bf16[64,2048]{1,0:T(8,128)(2,1)} %get-tuple-element.21.refs_0_, ...), custom_call_target="tpu_custom_call" | custom-call | tf_op jit(solution)/shard_map/finish/pallas_call | solution.py:438
